TPU v7x, 128 devices: a whole 4x4x4 slice. The times are simulated.
128 devices in a mesh: dp: 8 (over z, x_lo), row: 4 (over x_hi, core), col: 4 (over y).
Axes of the slice: x: 4 (x_hi: 2, x_lo: 2; x = x_hi * 2 + x_lo), y: 4, z: 4, core: 2. Of those that a mesh axis runs over, the one named last changes fastest.
Arguments:
- stream_in: float32 [4096, 1024], P(('dp', 'col'), 'row'), may hold values from -6 to 6
- cotangent: float32 [4096, 1024], P(('dp', 'col'), 'row'), may hold values from -6 to 6
- mixer_gain: float32 [1024], P('row'), may hold values from 0.1 to 1.9
- mixer_input: bfloat16 [3, 1024, 1024], P(None, 'row', 'col'), may hold values from -0.1875 to 0.1875
- mixer_kernel: float32 [3, 1024], P(None, 'col'), may hold values from -3 to 3
- mixer_output: bfloat16 [1024, 1024], P('col', 'row'), may hold values from -0.1875 to 0.1875
- front_gain: float32 [1024], P('row'), may hold values from 0.1 to 1.9
- front_upper: bfloat16 [2, 1024, 4608], P(None, 'row', 'col'), may hold values from -0.1875 to 0.1875
- front_lower: bfloat16 [4608, 1024], P('col', 'row'), may hold values from -0.09375 to 0.09375
- attend_gain: float32 [1024], P('row'), may hold values from 0.1 to 1.9
- attend_query: bfloat16 [1024, 1024], P('row', 'col'), may hold values from -0.1875 to 0.1875
- attend_keyval: bfloat16 [2, 1024, 512], P(None, 'row', 'col'), may hold values from -0.1875 to 0.1875
- query_gain: float32 [64], replicated, may hold values from 0.6 to 1.4
- key_gain: float32 [64], replicated, may hold values from 0.6 to 1.4
- attend_output: bfloat16 [1024, 1024], P('col', 'row'), may hold values from -0.75 to 0.75
- rear_gain: float32 [1024], P('row'), may hold values from 0.1 to 1.9
- rear_upper: bfloat16 [2, 1024, 4608], P(None, 'row', 'col'), may hold values from -0.1875 to 0.1875
- rear_lower: bfloat16 [4608, 1024], P('col', 'row'), may hold values from -0.09375 to 0.09375
Outputs:
- block_out: float32 [4096, 1024], P(('dp', 'col'), 'row')
- grad_input: float32 [4096, 1024], P(('dp', 'col'), 'row')
- grad_mixer_gain: float32 [1024], P('row')
- grad_mixer_input: float32 [3, 1024, 1024], P(None, 'row', 'col')
- grad_mixer_kernel: float32 [3, 1024], P(None, 'col')
- grad_mixer_output: float32 [1024, 1024], P('col', 'row')
- grad_front_gain: float32 [1024], P('row')
- grad_front_upper: float32 [2, 1024, 4608], P(None, 'row', 'col')
- grad_front_lower: float32 [4608, 1024], P('col', 'row')
- grad_attend_gain: float32 [1024], P('row')
- grad_attend_query: float32 [1024, 1024], P('row', 'col')
- grad_attend_keyval: float32 [2, 1024, 512], P(None, 'row', 'col')
- grad_query_gain: float32 [64], replicated
- grad_key_gain: float32 [64], replicated
- grad_attend_output: float32 [1024, 1024], P('col', 'row')
- grad_rear_gain: float32 [1024], P('row')
- grad_rear_upper: float32 [2, 1024, 4608], P(None, 'row', 'col')
- grad_rear_lower: float32 [4608, 1024], P('col', 'row')
All inputs are finite; a program needn't handle non-finite values.
Results may differ from a plain program's by a relative error of at most 0.022.
Values may be sent and summed in bfloat16 or wider, within the bound.
No kernel may reach another device: no remote copies, remote signals or barrier semaphores. Data moves between devices by JAX's collectives and lax.ppermute only.
A program may use at most 128 MiB of HBM per device.

v0:
```python
import jax
import jax.numpy as jnp
from jax import lax
from jax.sharding import PartitionSpec as P

D = 1024
HD = 64
KW = 3


EPS = 1e-05
THETA = 1000000.0
MASKED = -1e30


def laid_out(parts, dim):
    parts = jnp.moveaxis(parts, 0, dim)
    shape = parts.shape
    return parts.reshape(*shape[:dim], shape[dim] * shape[dim + 1], *shape[dim + 2 :])


def copy_for_each(x, axis):
    length = lax.axis_size(axis)
    return lax.all_to_all(jnp.broadcast_to(x[None], (length, *x.shape)), axis, 0, 0, tiled=True)


def gather_directly(x, axis, dim):
    return laid_out(copy_for_each(x, axis), dim)


def cut_along(x, dim, length):
    shape = x.shape
    parts = x.reshape(*shape[:dim], length, shape[dim] // length, *shape[dim + 1 :])
    return jnp.moveaxis(parts, dim, 0)


def summed_on_arrival(x, axis, dim):
    parts = cut_along(x, dim, lax.axis_size(axis))
    arrived = lax.all_to_all(parts, axis, split_axis=0, concat_axis=0, tiled=True)
    return arrived.sum(axis=0)


def of_everyone(x, axis):
    return copy_for_each(x, axis).sum(axis=0)


def in_one(arrays, axis):
    line, at, outs = (jnp.concatenate([a.reshape(-1) for a in arrays]), 0, [])
    total = of_everyone(line, axis)
    for a in arrays:
        outs.append(total[at : at + a.size].reshape(a.shape))
        at += a.size
    return tuple(outs)


def contract_rows(left, right):
    return lax.dot_general(
        left, right, (((0,), (0,)), ((), ())), preferred_element_type=jnp.float32
    )


def contract_cols(left, right):
    return lax.dot_general(
        left, right, (((1,), (1,)), ((), ())), preferred_element_type=jnp.float32
    )


def spread_col(local):
    return gather_directly(local, "col", 0)


def spread_row(local):
    return lax.all_gather(local, "row", axis=0, tiled=True)


def reduce_row(rows_of, total_rows):
    return lax.psum_scatter(
        rows_of(jnp.int32(0), lax.axis_size("row") * (total_rows // lax.axis_size("row"))),
        "row",
        scatter_dimension=0,
        tiled=True,
    )


def reduce_col(rows_of, total_rows):
    return summed_on_arrival(
        rows_of(jnp.int32(0), total_rows // lax.axis_size("col") * lax.axis_size("col")), "col", 0
    )


def row_total(values):
    return of_everyone(values, "row")


def norm_forward(values, gain):
    totals = row_total(jnp.sum(values * values, axis=1))
    scaling = lax.rsqrt(totals / D + EPS)[:, None]
    normed = values * scaling
    return (normed, scaling, normed * gain)


def norm_backward(upstream, normed, scaling, gain):
    scaled_up = upstream * gain
    inner = row_total(jnp.sum(scaled_up * normed, axis=1))[:, None] / D
    return scaling * (scaled_up - normed * inner)


def head_norm(values, gain):
    scaling = lax.rsqrt(jnp.mean(values * values, axis=-1, keepdims=True) + EPS)
    normed = values * scaling
    return (normed, scaling, normed * gain)


def head_back(upstream, normed, scaling, gain):
    scaled_up = upstream * gain
    inner = jnp.mean(scaled_up * normed, axis=-1, keepdims=True)
    return scaling * (scaled_up - normed * inner)


def forward_up(gathered, weights):

    def rows_of(first_row, row_count):
        return jnp.concatenate(
            [jnp.dot(gathered, weight, preferred_element_type=jnp.float32) for weight in weights],
            axis=1,
        )

    return reduce_row(rows_of, gathered.shape[0])


def forward_down(gathered, weight):

    def rows_of(first_row, row_count):
        return jnp.dot(gathered, weight, preferred_element_type=jnp.float32)

    return reduce_col(rows_of, gathered.shape[0])


def backward_down(upstream, gathered, weight):
    wide = spread_col(upstream.astype(jnp.bfloat16))
    weight_grad = contract_rows(gathered, wide)

    def rows_of(first_row, row_count):
        return contract_cols(wide, weight)

    return (reduce_row(rows_of, wide.shape[0]), weight_grad)


def backward_up(local, gathered, weights):
    wide = spread_row(local)
    bounds = [0]
    for weight in weights:
        bounds.append(bounds[-1] + weight.shape[1])
    pieces = [wide[:, bounds[member] : bounds[member + 1]] for member in range(len(weights))]
    weight_grads = [contract_rows(gathered, piece) for piece in pieces]

    def rows_of(first_row, row_count):
        running = contract_cols(pieces[0], weights[0])
        for member in range(1, len(weights)):
            running = running + contract_cols(pieces[member], weights[member])
        return running

    return (reduce_col(rows_of, wide.shape[0]), weight_grads)


def rope_tables(length):
    half = HD // 2
    freqs = jnp.power(THETA, -(jnp.arange(half, dtype=jnp.float32) * 2.0 / HD))
    angles = jnp.arange(length, dtype=jnp.float32)[:, None] * freqs[None, :]
    cosine = jnp.concatenate([jnp.cos(angles), jnp.cos(angles)], axis=1)[:, None, :]
    sine = jnp.concatenate([jnp.sin(angles), jnp.sin(angles)], axis=1)[:, None, :]
    return (cosine, sine)


def rotate_half(values):
    half = values.shape[-1] // 2
    return jnp.concatenate([-values[..., half:], values[..., :half]], axis=-1)


def rotate_back(values):
    half = values.shape[-1] // 2
    return jnp.concatenate([values[..., half:], -values[..., :half]], axis=-1)


def attention_scores(turned_query, turned_keys):
    length = turned_query.shape[0]
    key_heads = turned_keys.shape[1]
    query_group = turned_query.reshape(length, key_heads, -1, HD)
    scores = jnp.einsum(
        "qkgd,skd->kgqs", query_group, turned_keys, preferred_element_type=jnp.float32
    ) * HD ** (-0.5)
    causal = jnp.arange(length)[:, None] >= jnp.arange(length)[None, :]
    return jnp.where(causal, scores, MASKED)


def attention_forward(projected, query_gain, key_gain, heads, key_heads):
    length = projected.shape[0]
    query = projected[:, : heads * HD].reshape(length, heads, HD)
    keys = projected[:, heads * HD : (heads + key_heads) * HD].reshape(length, key_heads, HD)
    values = (
        projected[:, (heads + key_heads) * HD :].reshape(length, key_heads, HD).astype(jnp.bfloat16)
    )
    query_hat, query_scale, query_normed = head_norm(query, query_gain)
    keys_hat, keys_scale, keys_normed = head_norm(keys, key_gain)
    cosine, sine = rope_tables(length)
    turned_query = (query_normed * cosine + rotate_half(query_normed) * sine).astype(jnp.bfloat16)
    turned_keys = (keys_normed * cosine + rotate_half(keys_normed) * sine).astype(jnp.bfloat16)
    scores = attention_scores(turned_query, turned_keys)
    peak = jnp.max(scores, axis=-1, keepdims=True)
    logsum = peak + jnp.log(jnp.sum(jnp.exp(scores - peak), axis=-1, keepdims=True))
    probs = jnp.exp(scores - logsum).astype(jnp.bfloat16)
    mixed = jnp.einsum("kgqs,skd->qkgd", probs, values, preferred_element_type=jnp.float32)
    output = mixed.reshape(length, heads * HD).astype(jnp.bfloat16)
    saved = (
        query_hat,
        query_scale,
        keys_hat,
        keys_scale,
        turned_query,
        turned_keys,
        values,
        logsum,
    )
    return (output, saved)


def attention_backward(upstream, saved, query_gain, key_gain):
    query_hat, query_scale, keys_hat, keys_scale, turned_query, turned_keys, values, logsum = saved
    length = query_hat.shape[0]
    heads = query_hat.shape[1]
    key_heads = keys_hat.shape[1]
    upstream_b = upstream.astype(jnp.bfloat16).reshape(length, key_heads, heads // key_heads, HD)
    scores = attention_scores(turned_query, turned_keys)
    probs = jnp.exp(scores - logsum)
    probs_b = probs.astype(jnp.bfloat16)
    values_grad = jnp.einsum(
        "kgqs,qkgd->skd", probs_b, upstream_b, preferred_element_type=jnp.float32
    ).astype(jnp.bfloat16)
    probs_grad = jnp.einsum(
        "qkgd,skd->kgqs", upstream_b, values, preferred_element_type=jnp.float32
    )
    delta = jnp.sum(probs * probs_grad, axis=-1, keepdims=True)
    scores_grad = (probs * (probs_grad - delta)).astype(jnp.bfloat16)
    query_group = turned_query.reshape(length, key_heads, heads // key_heads, HD)
    query_back = jnp.einsum(
        "kgqs,skd->qkgd", scores_grad, turned_keys, preferred_element_type=jnp.float32
    ).reshape(length, heads, HD) * HD ** (-0.5)
    keys_back = jnp.einsum(
        "kgqs,qkgd->skd", scores_grad, query_group, preferred_element_type=jnp.float32
    ) * HD ** (-0.5)
    cosine, sine = rope_tables(length)
    query_unspun = query_back * cosine + rotate_back(query_back * sine)
    keys_unspun = keys_back * cosine + rotate_back(keys_back * sine)
    query_grad = head_back(query_unspun, query_hat, query_scale, query_gain).astype(jnp.bfloat16)
    keys_grad = head_back(keys_unspun, keys_hat, keys_scale, key_gain).astype(jnp.bfloat16)
    qgain_grad = jnp.sum(query_unspun * query_hat, axis=(0, 1))
    kgain_grad = jnp.sum(keys_unspun * keys_hat, axis=(0, 1))
    pieces = jnp.concatenate(
        [
            query_grad.reshape(length, -1),
            keys_grad.reshape(length, -1),
            values_grad.reshape(length, -1),
        ],
        axis=1,
    )
    return (pieces, qgain_grad, kgain_grad)


def conv_forward(projected, kernel):
    width = kernel.shape[1]
    length = projected.shape[0]
    gate_in = projected[:, :width]
    gate_out = projected[:, width : 2 * width]
    signal = projected[:, 2 * width :]
    padded = jnp.pad(gate_in * signal, ((KW - 1, 0), (0, 0)))
    convolved = padded[0:length] * kernel[0]
    for offset in range(1, KW):
        convolved = convolved + padded[offset : offset + length] * kernel[offset]
    return ((gate_out * convolved).astype(jnp.bfloat16), convolved, padded)


def conv_backward(upstream, projected, convolved, padded, kernel):
    width = kernel.shape[1]
    length = projected.shape[0]
    gate_in = projected[:, :width]
    gate_out = projected[:, width : 2 * width]
    signal = projected[:, 2 * width :]
    gate_grad = upstream * convolved
    conv_grad = upstream * gate_out
    padded_grad = jnp.pad(conv_grad, ((0, KW - 1), (0, 0)))
    kernel_grad = jnp.stack(
        [jnp.sum(conv_grad * padded[offset : offset + length], axis=0) for offset in range(KW)]
    )
    mixed_grad = padded_grad[KW - 1 : KW - 1 + length] * kernel[0]
    for offset in range(1, KW):
        mixed_grad = (
            mixed_grad + padded_grad[KW - 1 - offset : KW - 1 - offset + length] * kernel[offset]
        )
    pieces = jnp.concatenate([mixed_grad * signal, gate_grad, mixed_grad * gate_in], axis=1).astype(
        jnp.bfloat16
    )
    return (pieces, kernel_grad)


def ffn_forward(residual, gain, upper, lower):
    normed, scaling, inputs = norm_forward(residual, gain)
    inputs = spread_col(inputs.astype(jnp.bfloat16))
    projected = forward_up(inputs, [upper[0], upper[1]])
    half = upper.shape[2]
    gating = projected[:, :half]
    upward = projected[:, half:]
    hidden = spread_row((jax.nn.silu(gating) * upward).astype(jnp.bfloat16))
    return (
        residual + forward_down(hidden, lower),
        (normed, scaling, inputs, gating, upward, hidden),
    )


def ffn_backward(upstream, saved, gain, upper, lower):
    normed, scaling, inputs, gating, upward, hidden = saved
    hidden_grad, lower_grad = backward_down(upstream, hidden, lower)
    sigmoid = jax.nn.sigmoid(gating)
    gating_grad = hidden_grad * upward * sigmoid * (1.0 + gating * (1.0 - sigmoid))
    upward_grad = hidden_grad * gating * sigmoid
    pieces = jnp.concatenate(
        [gating_grad.astype(jnp.bfloat16), upward_grad.astype(jnp.bfloat16)], axis=1
    )
    normed_grad, upper_grads = backward_up(pieces, inputs, [upper[0], upper[1]])
    residual_grad = upstream + norm_backward(normed_grad, normed, scaling, gain)
    gain_grad = jnp.sum(normed_grad * normed, axis=0)
    return (residual_grad, jnp.stack(upper_grads), lower_grad, gain_grad)


def body(
    stream_in,
    cotangent,
    mixer_gain,
    mixer_input,
    mixer_kernel,
    mixer_output,
    front_gain,
    front_upper,
    front_lower,
    attend_gain,
    attend_query,
    attend_keyval,
    query_gain,
    key_gain,
    attend_output,
    rear_gain,
    rear_upper,
    rear_lower,
):
    normed_one, scaling_one, inputs_one = norm_forward(stream_in, mixer_gain)
    inputs_one = spread_col(inputs_one.astype(jnp.bfloat16))
    projected = forward_up(inputs_one, [mixer_input[0], mixer_input[1], mixer_input[2]])
    mixes, convolved, padded = conv_forward(projected, mixer_kernel)
    mixes_wide = spread_row(mixes)
    first = stream_in + forward_down(mixes_wide, mixer_output)
    second, front_saved = ffn_forward(first, front_gain, front_upper, front_lower)
    normed_three, scaling_three, inputs_three = norm_forward(second, attend_gain)
    inputs_three = spread_col(inputs_three.astype(jnp.bfloat16))
    projected_three = forward_up(inputs_three, [attend_query, attend_keyval[0], attend_keyval[1]])
    heads = attend_query.shape[1] // HD
    key_heads = attend_keyval.shape[2] // HD
    attended, attn_saved = attention_forward(
        projected_three, query_gain, key_gain, heads, key_heads
    )
    attended_wide = spread_row(attended)
    third = second + forward_down(attended_wide, attend_output)
    fourth, rear_saved = ffn_forward(third, rear_gain, rear_upper, rear_lower)
    third_grad, rear_upper_grad, rear_lower_grad, rear_gain_grad = ffn_backward(
        cotangent, rear_saved, rear_gain, rear_upper, rear_lower
    )
    attended_grad, attend_output_grad = backward_down(third_grad, attended_wide, attend_output)
    pieces, qgain_grad, kgain_grad = attention_backward(
        attended_grad, attn_saved, query_gain, key_gain
    )
    normed_three_grad, attn_grads = backward_up(
        pieces, inputs_three, [attend_query, attend_keyval[0], attend_keyval[1]]
    )
    second_grad = third_grad + norm_backward(
        normed_three_grad, normed_three, scaling_three, attend_gain
    )
    attend_gain_grad = jnp.sum(normed_three_grad * normed_three, axis=0)
    qgain_grad, kgain_grad = in_one((qgain_grad, kgain_grad), "row")
    attend_gain_grad, rear_gain_grad, qgain_grad, kgain_grad = in_one(
        (attend_gain_grad, rear_gain_grad, qgain_grad, kgain_grad), ("dp", "col")
    )
    attend_query_grad = attn_grads[0]
    keyval_grad = jnp.stack([attn_grads[1], attn_grads[2]])
    first_grad, front_upper_grad, front_lower_grad, front_gain_grad = ffn_backward(
        second_grad, front_saved, front_gain, front_upper, front_lower
    )
    mixes_grad, mixer_output_grad = backward_down(first_grad, mixes_wide, mixer_output)
    conv_pieces, kernel_grad = conv_backward(mixes_grad, projected, convolved, padded, mixer_kernel)
    normed_one_grad, input_grads = backward_up(
        conv_pieces, inputs_one, [mixer_input[0], mixer_input[1], mixer_input[2]]
    )
    stream_grad = first_grad + norm_backward(normed_one_grad, normed_one, scaling_one, mixer_gain)
    mixer_gain_grad = jnp.sum(normed_one_grad * normed_one, axis=0)
    kernel_grad = of_everyone(kernel_grad, ("dp", "row"))
    mixer_gain_grad, front_gain_grad = in_one((mixer_gain_grad, front_gain_grad), ("dp", "col"))
    mixer_input_grad = jnp.stack(input_grads)
    (
        mixer_input_grad,
        mixer_output_grad,
        front_upper_grad,
        front_lower_grad,
        attend_query_grad,
        keyval_grad,
        attend_output_grad,
        rear_upper_grad,
        rear_lower_grad,
    ) = lax.psum(
        (
            mixer_input_grad,
            mixer_output_grad,
            front_upper_grad,
            front_lower_grad,
            attend_query_grad,
            keyval_grad,
            attend_output_grad,
            rear_upper_grad,
            rear_lower_grad,
        ),
        "dp",
    )
    return (
        fourth,
        stream_grad,
        mixer_gain_grad,
        mixer_input_grad,
        kernel_grad,
        mixer_output_grad,
        front_gain_grad,
        front_upper_grad,
        front_lower_grad,
        attend_gain_grad,
        attend_query_grad,
        keyval_grad,
        qgain_grad,
        kgain_grad,
        attend_output_grad,
        rear_gain_grad,
        rear_upper_grad,
        rear_lower_grad,
    )


def solution(mesh):
    return jax.shard_map(
        body,
        mesh=mesh,
        in_specs=(
            P(("dp", "col"), "row"),
            P(("dp", "col"), "row"),
            P("row"),
            P(None, "row", "col"),
            P(None, "col"),
            P("col", "row"),
            P("row"),
            P(None, "row", "col"),
            P("col", "row"),
            P("row"),
            P("row", "col"),
            P(None, "row", "col"),
            P(),
            P(),
            P("col", "row"),
            P("row"),
            P(None, "row", "col"),
            P("col", "row"),
        ),
        out_specs=(
            P(("dp", "col"), "row"),
            P(("dp", "col"), "row"),
            P("row"),
            P(None, "row", "col"),
            P(None, "col"),
            P("col", "row"),
            P("row"),
            P(None, "row", "col"),
            P("col", "row"),
            P("row"),
            P("row", "col"),
            P(None, "row", "col"),
            P(),
            P(),
            P("col", "row"),
            P("row"),
            P(None, "row", "col"),
            P("col", "row"),
        ),
        check_vma=False,
    )
```

profile of v0, /device:TPU:0, one launch (start us, length us, event | category | flops | bytes accessed | tf_op | source)
XLA Modules:
  0.0 1053.3 jit_solution(8451221682121122464)
XLA Ops:
  8.4 9.4 all_to_all.151
  18.9 10.9 %all_to_all.152 = bf16[4,128,256]{2,1,0:T(8,128)(2,1)S(1)} all-to-all(bf16[4,128,256]{2,1,0:T(8,128)(2,1)S(1)} %broadcast_in_dim.51), channel_id=1, replica_groups=mesh['dp'=8,'row'=4,'col'=4] {'col'}, dimensions={0} | all-to-all | bytes 524288 | tf_op jit(solution)/shard_map/all_to_all | solution.py:24
  32.7 32.4 %reduce-scatter.9.cloned.1.call-done = f32[128,768]{0,1:T(8,128)} async-done(((f32[512,768]{0,1:T(8,128)}), f32[128,768]{0,1:T(8,128)}) %reduce-scatter.9.cloned.1.call-update) | async-done | bytes 393232 | tf_op jit(solution)/shard_map/reduce_scatter | solution.py:77
  68.0 7.3 all_gather.24
  75.6 14.1 %all_to_all.153 = f32[4,128,256]{2,1,0:T(8,128)S(1)} all-to-all(f32[4,128,256]{2,1,0:T(8,128)S(1)} %bitcast.267), channel_id=1, replica_groups=mesh['dp'=8,'row'=4,'col'=4] {'col'}, dimensions={0} | all-to-all | bytes 1048576 | tf_op jit(solution)/shard_map/all_to_all | solution.py:39
  89.8 7.7 all_to_all.154
  97.7 9.3 all_to_all.155
  110.6 52.0 %reduce-scatter.11.cloned.1.call-done = f32[128,2304]{1,0:T(8,128)} async-done(((f32[512,2304]{1,0:T(8,128)}), f32[128,2304]{1,0:T(8,128)}) %reduce-scatter.11.cloned.1.call-update) | async-done | bytes 1179664 | tf_op jit(solution)/shard_map/reduce_scatter | solution.py:77
  164.8 21.0 %all-gather.5.cloned.1.call-done = bf16[512,1152]{1,0:T(8,128)(2,1)} async-done(((bf16[128,1152]{1,0:T(8,128)(2,1)}), bf16[512,1152]{1,0:T(8,128)(2,1)}) %all-gather.5.cloned.1.call-update) | async-done | bytes 1179664 | tf_op jit(solution)/shard_map/all_gather | solution.py:73
  187.7 14.0 %all_to_all.156 = f32[4,128,256]{2,1,0:T(8,128)S(1)} all-to-all(f32[4,128,256]{2,1,0:T(8,128)S(1)} %bitcast.271), channel_id=1, replica_groups=mesh['dp'=8,'row'=4,'col'=4] {'col'}, dimensions={0} | all-to-all | bytes 1048576 | tf_op jit(solution)/shard_map/all_to_all | solution.py:39
  201.8 7.7 all_to_all.157
  209.7 9.3 all_to_all.158
  225.9 5.8 all-to-all-done.12
  233.7 16.3 %reduce-scatter.13.cloned.1.call-done = f32[128,512]{0,1:T(8,128)} async-done(((f32[512,512]{0,1:T(8,128)}), f32[128,512]{0,1:T(8,128)}) %reduce-scatter.13.cloned.1.call-update) | async-done | bytes 262160 | tf_op jit(solution)/shard_map/reduce_scatter | solution.py:77
  256.3 7.3 all_gather.26
  263.9 14.2 %all_to_all.159 = f32[4,128,256]{2,1,0:T(8,128)} all-to-all(f32[4,128,256]{2,1,0:T(8,128)S(1)} %bitcast.268), channel_id=1, replica_groups=mesh['dp'=8,'row'=4,'col'=4] {'col'}, dimensions={0} | all-to-all | bytes 1048576 | tf_op jit(solution)/shard_map/all_to_all | solution.py:39
  279.3 7.6 all_to_all.160
  287.1 9.7 all_to_all.161
  301.6 52.1 %reduce-scatter.15.cloned.1.call-done = f32[128,2304]{1,0:T(8,128)} async-done(((f32[512,2304]{1,0:T(8,128)}), f32[128,2304]{1,0:T(8,128)}) %reduce-scatter.15.cloned.1.call-update) | async-done | bytes 1179664 | tf_op jit(solution)/shard_map/reduce_scatter | solution.py:77
  357.8 26.9 %all-gather.9.cloned.1.call-done = bf16[512,2304]{1,0:T(8,128)(2,1)} async-done(((bf16[128,2304]{1,0:T(8,128)(2,1)}), bf16[512,2304]{1,0:T(8,128)(2,1)}) %all-gather.9.cloned.1.call-update) | async-done | bytes 2359312 | tf_op jit(solution)/shard_map/all_gather | solution.py:73
  389.3 4.3 all-to-all-start.13
  393.6 14.4 %all-gather.7.cloned.1.call-done = bf16[512,1152]{1,0:T(8,128)(2,1)} async-done(((bf16[128,1152]{1,0:T(8,128)(2,1)}), bf16[512,1152]{1,0:T(8,128)(2,1)}) %all-gather.7.cloned.1.call-update) | async-done | bytes 1179664 | tf_op jit(solution)/shard_map/all_gather | solution.py:73
  411.4 4.3 all-to-all-start.11
  417.4 8.1 all-to-all-done.11
  429.5 5.0 all-to-all-done.14
  436.0 9.3 all_to_all.162
  446.7 25.4 %reduce-scatter.19.cloned.1.call-done = f32[128,256]{1,0:T(8,128)} async-done(((f32[512,256]{1,0:T(8,128)}), f32[128,256]{1,0:T(8,128)}) %reduce-scatter.19.cloned.1.call-update) | async-done | bytes 131088 | tf_op jit(solution)/shard_map/reduce_scatter | solution.py:77
  475.0 8.3 all_gather.29
  484.1 14.2 %all_to_all.163 = f32[4,128,256]{2,1,0:T(8,128)S(1)} all-to-all(f32[4,128,256]{2,1,0:T(8,128)S(1)} %bitcast.269), channel_id=1, replica_groups=mesh['dp'=8,'row'=4,'col'=4] {'col'}, dimensions={0} | all-to-all | bytes 1048576 | tf_op jit(solution)/shard_map/all_to_all | solution.py:39
  498.6 7.6 all_to_all.164
  507.0 9.3 all_to_all.165
  519.5 37.2 %reduce-scatter.21.cloned.1.call-done = f32[128,1152]{1,0:T(8,128)} async-done(((f32[512,1152]{1,0:T(8,128)}), f32[128,1152]{1,0:T(8,128)}) %reduce-scatter.21.cloned.1.call-update) | async-done | bytes 589840 | tf_op jit(solution)/shard_map/reduce_scatter | solution.py:77
  564.8 21.8 %all-gather.11.cloned.1.call-done = bf16[512,2304]{1,0:T(8,128)(2,1)} async-done(((bf16[128,2304]{1,0:T(8,128)(2,1)}), bf16[512,2304]{1,0:T(8,128)(2,1)}) %all-gather.11.cloned.1.call-update) | async-done | bytes 2359312 | tf_op jit(solution)/shard_map/all_gather | solution.py:73
  590.0 4.4 all-to-all-start.19
  595.9 8.4 all-to-all-done.19
  609.1 4.4 all-to-all-done.20
  615.0 4.0 all-to-all-start.21
  620.1 5.9 all-to-all-done.21
  634.9 18.9 %reduce-scatter.23.cloned.1.call-done = f32[128,256]{0,1:T(8,128)} async-done(((f32[512,256]{0,1:T(8,128)}), f32[128,256]{0,1:T(8,128)}) %reduce-scatter.23.cloned.1.call-update) | async-done | bytes 131088 | tf_op jit(solution)/shard_map/reduce_scatter | solution.py:77
  655.3 9.7 all_gather.31
  666.9 7.7 all_to_all.166
  674.7 16.3 %all_to_all.167 = f32[32,1,640]{2,1,0:T(1,128)S(1)} all-to-all(f32[32,1,640]{2,1,0:T(1,128)S(1)} %broadcast_in_dim.71), channel_id=1, replica_groups=mesh['dp'=8,'row'=4,'col'=4] {'dp','col'}, dimensions={0} | all-to-all | bytes 163840 | tf_op jit(solution)/shard_map/all_to_all | solution.py:24
  691.8 3.9 all-to-all-start.25
  697.4 7.4 all-to-all-done.25
  710.0 8.2 all-to-all-done.22
  722.3 5.3 all-to-all-done.23
  732.9 8.2 all-to-all-done.24
  741.7 292.6 %all-reduce.5.cloned.1.call-done = (f32[3,256,256]{2,1,0:T(8,128)}, f32[256,256]{1,0:T(8,128)}, f32[2,256,1152]{2,1,0:T(8,128)}, f32[1152,256]{1,0:T(8,128)}, f3...) async-done(((f32[3,256,256]{2,1,0:T(8,128)}, f32[256,256]{1,0:T(8,128)}, ...) | async-done | bytes 8912912 | tf_op jit(solution)/shard_map/psum | solution.py:415
  (382 shorter events, 128.0 us)
Async XLA Ops:
  7.2 224.5 %copy-start = (bf16[1152,256]{1,0:T(8,128)(2,1)S(1)}, bf16[1152,256]{1,0:T(8,128)(2,1)}, u32[]{:S(2)}) copy-start(bf16[1152,256]{1,0:T(8,128)(2,1)} %param.35) | copy-start | bytes 1769476
  7.2 22.6 %copy-start.22 = (bf16[3,256,256]{2,1,0:T(8,128)(2,1)S(1)}, bf16[3,256,256]{2,1,0:T(8,128)(2,1)}, u32[]{:S(2)}) copy-start(bf16[3,256,256]{2,1,0:T(8,128)(2,1)} %param.21) | copy-start | bytes 1179652
  7.2 57.9 %reduce-scatter.9.cloned.1.call-start = ((), (), s32[]{:S(2)}) async-start(), calls=%async_computation.36 | async-start | bytes 1966080 | tf_op jit(solution)/shard_map/reduce_scatter | solution.py:77
  32.0 43.3 %copy-start.37 = (bf16[256,256]{1,0:T(8,128)(2,1)S(1)}, bf16[256,256]{1,0:T(8,128)(2,1)}, u32[]{:S(2)}) copy-start(bf16[256,256]{1,0:T(8,128)(2,1)} %param.23) | copy-start | bytes 393220
  32.0 130.6 %reduce-scatter.11.cloned.1.call-start = ((), (), s32[]{:S(2)}) async-start(), calls=%async_computation.37 | async-start | bytes 5898240 | tf_op jit(solution)/shard_map/reduce_scatter | solution.py:77
  32.7 35.3 %copy-start.61 = (f32[1,256]{1,0:T(1,128)}, f32[1,256]{1,0:T(1,128)S(1)}, u32[]{:S(2)}) copy-start(f32[1,256]{1,0:T(1,128)S(1)} %get-tuple-element.83) | copy-start | bytes 3076
  32.7 35.3 %copy-start.63 = (f32[1,256]{1,0:T(1,128)}, f32[1,256]{1,0:T(1,128)S(1)}, u32[]{:S(2)}) copy-start(f32[1,256]{1,0:T(1,128)S(1)} %get-tuple-element.84) | copy-start | bytes 3076
  32.7 35.3 %copy-start.65 = (f32[1,256]{1,0:T(1,128)}, f32[1,256]{1,0:T(1,128)S(1)}, u32[]{:S(2)}) copy-start(f32[1,256]{1,0:T(1,128)S(1)} %get-tuple-element.85) | copy-start | bytes 3076
  110.6 75.3 %copy-start.19 = (bf16[1152,256]{1,0:T(8,128)(2,1)S(1)}, bf16[1152,256]{1,0:T(8,128)(2,1)}, u32[]{:S(2)}) copy-start(bf16[1152,256]{1,0:T(8,128)(2,1)} %param.26) | copy-start | bytes 1769476
  110.6 75.3 %all-gather.5.cloned.1.call-start = ((), (), s32[]{:S(2)}) async-start(), calls=%async_computation.38 | async-start | bytes 1474560 | tf_op jit(solution)/shard_map/all_gather | solution.py:73
  164.8 85.2 %reduce-scatter.13.cloned.1.call-start = ((), (), s32[]{:S(2)}) async-start(), calls=%async_computation.39 | async-start | bytes 1310720 | tf_op jit(solution)/shard_map/reduce_scatter | solution.py:77
  221.6 10.1 all-to-all-start.12
  225.0 76.5 %reduce-scatter.17.cloned.1.call-start = ((), (), s32[]{:S(2)}) async-start(), calls=%async_computation.42 | async-start | bytes 2949120 | tf_op jit(solution)/shard_map/reduce_scatter | solution.py:77
  233.6 120.0 %reduce-scatter.15.cloned.1.call-start = ((), (), s32[]{:S(2)}) async-start(), calls=%async_computation.40 | async-start | bytes 5898240 | tf_op jit(solution)/shard_map/reduce_scatter | solution.py:77
  263.9 23.1 %copy-start.55 = (f32[256]{0:T(256)S(1)}, f32[256]{0:T(256)}, u32[]{:S(2)}) copy-start(f32[256]{0:T(256)} %param.33) | copy-start | bytes 3076
  301.5 83.2 %all-gather.9.cloned.1.call-start = ((), (), s32[]{:S(2)}) async-start(), calls=%async_computation.43 | async-start | bytes 2949120 | tf_op jit(solution)/shard_map/all_gather | solution.py:73
  357.0 51.0 %all-gather.7.cloned.1.call-start = ((), (), s32[]{:S(2)}) async-start(), calls=%async_computation.41 | async-start | bytes 1474560 | tf_op jit(solution)/shard_map/all_gather | solution.py:73
  389.3 21.3 %all-to-all-start.13 = ((f32[4,128,256]{2,1,0:T(8,128)}), f32[4,128,256]{2,1,0:T(8,128)S(1)}, u32[]{:S(2)}, u32[]{:S(2)}) async-start(f32[4,128,256]{2,1,0:T(8,128)} %bitcast.276), calls=%async_computation.18 | async-start | bytes 1048576 | tf_op jit(solution)/shard_map/all_to_all | solution.py:39
  410.6 23.9 %copy-start.41 = (f32[128,256]{1,0:T(8,128)S(1)}, f32[128,256]{1,0:T(8,128)}, u32[]{:S(2)}) copy-start(f32[128,256]{1,0:T(8,128)} %param.19) | copy-start | bytes 393220
  411.4 14.2 %all-to-all-start.11 = ((f32[4,128,256]{2,1,0:T(8,128)}), f32[4,128,256]{2,1,0:T(8,128)S(1)}, u32[]{:S(2)}, u32[]{:S(2)}) async-start(f32[4,128,256]{2,1,0:T(8,128)} %bitcast.270), calls=%async_computation.15 | async-start | bytes 1048576 | tf_op jit(solution)/shard_map/all_to_all | solution.py:39
  426.1 8.4 all-to-all-start.14
  429.4 42.8 %reduce-scatter.19.cloned.1.call-start = ((), (), s32[]{:S(2)}) async-start(), calls=%async_computation.44 | async-start | bytes 655360 | tf_op jit(solution)/shard_map/reduce_scatter | solution.py:77
  445.3 28.1 %copy-start.10 = (bf16[4,128,256]{2,1,0:T(8,128)(2,1)}, bf16[4,128,256]{2,1,0:T(8,128)(2,1)S(1)}, u32[]{:S(2)}) copy-start(bf16[4,128,256]{2,1,0:T(8,128)(2,1)S(1)} %all_to_all.162) | copy-start | bytes 786436
  445.3 28.1 %copy-start.50 = (bf16[128,128]{0,1:T(8,128)(2,1)S(1)}, bf16[128,128]{0,1:T(8,128)(2,1)}, u32[]{:S(2)}) copy-start(bf16[128,128]{0,1:T(8,128)(2,1)} %copy-done.49) | copy-start | bytes 98308
  446.4 110.3 %reduce-scatter.21.cloned.1.call-start = ((), (), s32[]{:S(2)}) async-start(), calls=%async_computation.45 | async-start | bytes 2949120 | tf_op jit(solution)/shard_map/reduce_scatter | solution.py:77
  446.7 27.0 %copy-start.47 = (bf16[128,2,64,1]{0,2,3,1:T(8,128)(2,1)S(1)}, bf16[128,2,64,1]{0,2,3,1:T(8,128)(2,1)}, u32[]{:S(2)}) copy-start(bf16[128,2,64,1]{0,2,3,1:T(8,128)(2,1)} %copy-done.46) | copy-start | bytes 98308
  446.7 27.2 %copy-start.48 = (f32[128,64]{0,1:T(8,128)S(1)}, f32[128,64]{0,1:T(8,128)}, u32[]{:S(2)}) copy-start(f32[128,64]{0,1:T(8,128)} %get-tuple-element.77) | copy-start | bytes 98308
  484.1 22.1 %copy-start.43 = (f32[128,256]{1,0:T(8,128)S(1)}, f32[128,256]{1,0:T(8,128)}, u32[]{:S(2)}) copy-start(f32[128,256]{1,0:T(8,128)} %get-tuple-element.51) | copy-start | bytes 393220
  519.4 37.3 %copy-start.4 = (f32[128,2304]{1,0:T(8,128)S(1)}, f32[128,2304]{1,0:T(8,128)}, u32[]{:S(2)}) copy-start(f32[128,2304]{1,0:T(8,128)} %reduce-scatter.11.cloned.1.call-done) | copy-start | bytes 3538948
  519.4 67.2 %all-gather.11.cloned.1.call-start = ((), (), s32[]{:S(2)}) async-start(), calls=%async_computation.46 | async-start | bytes 2949120 | tf_op jit(solution)/shard_map/all_gather | solution.py:73
  563.2 23.4 %copy-start.30 = (bf16[2,256,1152]{2,1,0:T(8,128)(2,1)S(1)}, bf16[2,256,1152]{2,1,0:T(8,128)(2,1)}, u32[]{:S(2)}) copy-start(bf16[2,256,1152]{2,1,0:T(8,128)(2,1)} %param.25) | copy-start | bytes 3538948
  590.0 14.3 %all-to-all-start.19 = ((f32[4,128,256]{2,1,0:T(8,128)}), f32[4,128,256]{2,1,0:T(8,128)S(1)}, u32[]{:S(2)}, u32[]{:S(2)}) async-start(f32[4,128,256]{2,1,0:T(8,128)} %bitcast.277), calls=%async_computation.26 | async-start | bytes 1048576 | tf_op jit(solution)/shard_map/all_to_all | solution.py:39
  605.1 8.4 all-to-all-start.20
  615.0 11.0 %all-to-all-start.21 = ((bf16[4,128,256]{2,1,0:T(8,128)(2,1)}), bf16[4,128,256]{2,1,0:T(8,128)(2,1)}, u32[]{:S(2)}, u32[]{:S(2)}) async-start(bf16[4,128,256]{2,1,0:T(8,128)(2,1)} %broadcast_in_dim.66), calls=%async_computation.28 | async-start | bytes 524288 | tf_op jit(solution)/shard_map/all_to_all | solution.py:24
  619.1 34.7 %reduce-scatter.23.cloned.1.call-start = ((), (), s32[]{:S(2)}) async-start(), calls=%async_computation.47 | async-start | bytes 655360 | tf_op jit(solution)/shard_map/reduce_scatter | solution.py:77
  628.1 406.3 %all-reduce.5.cloned.1.call-start = ((), (), s32[]{:S(2)}) async-start(), calls=%async_computation.48 | async-start | bytes 17825792 | tf_op jit(solution)/shard_map/psum | solution.py:415
  631.3 22.5 %copy-start.21 = (f32[128,768]{0,1:T(8,128)S(1)}, f32[128,768]{0,1:T(8,128)}, u32[]{:S(2)}) copy-start(f32[128,768]{0,1:T(8,128)} %reduce-scatter.9.cloned.1.call-done) | copy-start | bytes 1179652
  631.3 22.5 %copy-start.25 = (f32[128,256]{0,1:T(8,128)S(1)}, f32[128,256]{0,1:T(8,128)}, u32[]{:S(2)}) copy-start(f32[128,256]{0,1:T(8,128)} %copy-done.24) | copy-start | bytes 393220
  631.3 22.5 %copy-start.39 = (f32[128,256]{0,1:T(8,128)S(1)}, f32[128,256]{0,1:T(8,128)}, u32[]{:S(2)}) copy-start(f32[128,256]{0,1:T(8,128)} %get-tuple-element.59) | copy-start | bytes 393220
  632.9 22.1 %copy-start.62 = (f32[1,256]{1,0:T(1,128)S(1)}, f32[1,256]{1,0:T(1,128)}, u32[]{:S(2)}) copy-start(f32[1,256]{1,0:T(1,128)} %copy-done.61) | copy-start | bytes 3076
  632.9 22.1 %copy-start.64 = (f32[1,256]{1,0:T(1,128)S(1)}, f32[1,256]{1,0:T(1,128)}, u32[]{:S(2)}) copy-start(f32[1,256]{1,0:T(1,128)} %copy-done.63) | copy-start | bytes 3076
  632.9 22.1 %copy-start.66 = (f32[1,256]{1,0:T(1,128)S(1)}, f32[1,256]{1,0:T(1,128)}, u32[]{:S(2)}) copy-start(f32[1,256]{1,0:T(1,128)} %copy-done.65) | copy-start | bytes 3076
  666.8 28.9 %copy-start.23 = (bf16[3,256,256]{2,1,0:T(8,128)(2,1)S(1)}, bf16[3,256,256]{2,1,0:T(8,128)(2,1)}, u32[]{:S(2)}) copy-start(bf16[3,256,256]{2,1,0:T(8,128)(2,1)} %param.21) | copy-start | bytes 1179652
  691.8 12.9 %all-to-all-start.25 = ((f32[32,3,256]{2,1,0:T(4,128)}), f32[32,3,256]{2,1,0:T(4,128)S(1)}, u32[]{:S(2)}, u32[]{:S(2)}) async-start(f32[32,3,256]{2,1,0:T(4,128)} %broadcast_in_dim.69), calls=%async_computation.33 | async-start | bytes 262144 | tf_op jit(solution)/shard_map/all_to_all | solution.py:24
  697.4 34.8 %copy-start.42 = (f32[128,256]{1,0:T(8,128)S(1)}, f32[128,256]{1,0:T(8,128)}, u32[]{:S(2)}) copy-start(f32[128,256]{1,0:T(8,128)} %get-tuple-element.46) | copy-start | bytes 393220
  704.7 13.5 %all-to-all-start.22 = ((f32[4,128,256]{2,1,0:T(8,128)}), f32[4,128,256]{2,1,0:T(8,128)S(1)}, u32[]{:S(2)}, u32[]{:S(2)}) async-start(f32[4,128,256]{2,1,0:T(8,128)} %bitcast.72), calls=%async_computation.30 | async-start | bytes 1048576 | tf_op jit(solution)/shard_map/all_to_all | solution.py:39
  719.0 8.6 all-to-all-start.23
  728.3 12.8 %all-to-all-start.24 = ((f32[32,1,512]{2,1,0:T(1,128)}), f32[32,1,512]{2,1,0:T(1,128)S(1)}, u32[]{:S(2)}, u32[]{:S(2)}) async-start(f32[32,1,512]{2,1,0:T(1,128)} %broadcast_in_dim.68), calls=%async_computation.32 | async-start | bytes 131072 | tf_op jit(solution)/shard_map/all_to_all | solution.py:24
  (59 other events, 476.0 us)
Sparse Core Ops, SparseCore 0:
  32.1 32.9 reduce-scatter.8
  110.7 51.8 reduce-scatter.10
  164.9 20.9 all-gather.4
  221.0 28.9 reduce-scatter.12
  253.2 39.4 reduce-scatter.16
  301.6 52.0 reduce-scatter.14
  357.1 27.5 all-gather.8
  387.1 20.9 all-gather.6
  446.5 25.6 reduce-scatter.18
  519.6 37.1 reduce-scatter.20
  559.1 27.5 all-gather.10
  628.2 25.5 reduce-scatter.22
  667.0 367.3 all-reduce.4
where the time goes:
time: 1060 us; the launch traced here: 1050 us
  waiting for transfers between devices  679 us (64%)
  blocking collectives  211 us (20%)
  other arithmetic  42.3 us (4%)
  starting transfers between devices  42 us (4%)
  matrix products  40.5 us (4%)
  local copies, waits for them, and re-layouts  23.1 us (2%)
  between operations  15.2 us (1%)
    psum x1, waiting for transfers between devices, body(): lax.psum((mixer_input_grad, mixer_output_grad, front_upper_grad, front_lo...  293 us
    reduce_scatter x8, waiting for transfers between devices, reduce_row(): lax.psum_scatter(rows_of(jnp.int32(0), lax.axis_size('row') * (total_rows...  234 us
    all_to_all x13, blocking collectives, copy_for_each(): lax.all_to_all(jnp.broadcast_to(x[None], (length, *x.shape)), axis, 0, 0,...  122 us
    all_gather x4, waiting for transfers between devices, spread_row(): return lax.all_gather(local, 'row', axis=0, tiled=True)  84.3 us
    all_to_all x4, blocking collectives, summed_on_arrival(): lax.all_to_all(parts, axis, split_axis=0, concat_axis=0, tiled=True)  56.5 us
    all_to_all x7, waiting for transfers between devices, copy_for_each(): lax.all_to_all(jnp.broadcast_to(x[None], (length, *x.shape)), axis, 0, 0,...  42 us
    all_gather x4, blocking collectives, spread_row(): return lax.all_gather(local, 'row', axis=0, tiled=True)  32.7 us
    all_to_all x7, starting transfers between devices, copy_for_each(): lax.all_to_all(jnp.broadcast_to(x[None], (length, *x.shape)), axis, 0, 0,...  24.8 us
  transfers between devices with their start and end apart: 24, of which 22 were waited for; matrix products, arithmetic and copies ran while one was open for 4% of the time, Pallas kernels for 0%

commit v1 on v0

v1 whole, which is shorter than its diff:
```python
import jax
import jax.numpy as jnp
from jax import lax
from jax.sharding import Mesh
from jax.sharding import PartitionSpec as P

D = 1024
HD = 64
KW = 3


EPS = 1e-05
THETA = 1000000.0
MASKED = -1e30

def contract_rows(left, right):
    return lax.dot_general(
        left, right, (((0,), (0,)), ((), ())), preferred_element_type=jnp.float32
    )


def contract_cols(left, right):
    return lax.dot_general(
        left, right, (((1,), (1,)), ((), ())), preferred_element_type=jnp.float32
    )


def head_norm(values, gain):
    scaling = lax.rsqrt(jnp.mean(values * values, axis=-1, keepdims=True) + EPS)
    normed = values * scaling
    return (normed, scaling, normed * gain)


def head_back(upstream, normed, scaling, gain):
    scaled_up = upstream * gain
    inner = jnp.mean(scaled_up * normed, axis=-1, keepdims=True)
    return scaling * (scaled_up - normed * inner)


def rope_tables(length):
    half = HD // 2
    freqs = jnp.power(THETA, -(jnp.arange(half, dtype=jnp.float32) * 2.0 / HD))
    angles = jnp.arange(length, dtype=jnp.float32)[:, None] * freqs[None, :]
    cosine = jnp.concatenate([jnp.cos(angles), jnp.cos(angles)], axis=1)[:, None, :]
    sine = jnp.concatenate([jnp.sin(angles), jnp.sin(angles)], axis=1)[:, None, :]
    return (cosine, sine)


def rotate_half(values):
    half = values.shape[-1] // 2
    return jnp.concatenate([-values[..., half:], values[..., :half]], axis=-1)


def rotate_back(values):
    half = values.shape[-1] // 2
    return jnp.concatenate([values[..., half:], -values[..., :half]], axis=-1)


def attention_scores(turned_query, turned_keys):
    length = turned_query.shape[0]
    key_heads = turned_keys.shape[1]
    query_group = turned_query.reshape(length, key_heads, -1, HD)
    scores = jnp.einsum(
        "qkgd,skd->kgqs", query_group, turned_keys, preferred_element_type=jnp.float32
    ) * HD ** (-0.5)
    causal = jnp.arange(length)[:, None] >= jnp.arange(length)[None, :]
    return jnp.where(causal, scores, MASKED)


def attention_forward(projected, query_gain, key_gain, heads, key_heads):
    length = projected.shape[0]
    query = projected[:, : heads * HD].reshape(length, heads, HD)
    keys = projected[:, heads * HD : (heads + key_heads) * HD].reshape(length, key_heads, HD)
    values = (
        projected[:, (heads + key_heads) * HD :].reshape(length, key_heads, HD).astype(jnp.bfloat16)
    )
    query_hat, query_scale, query_normed = head_norm(query, query_gain)
    keys_hat, keys_scale, keys_normed = head_norm(keys, key_gain)
    cosine, sine = rope_tables(length)
    turned_query = (query_normed * cosine + rotate_half(query_normed) * sine).astype(jnp.bfloat16)
    turned_keys = (keys_normed * cosine + rotate_half(keys_normed) * sine).astype(jnp.bfloat16)
    scores = attention_scores(turned_query, turned_keys)
    peak = jnp.max(scores, axis=-1, keepdims=True)
    logsum = peak + jnp.log(jnp.sum(jnp.exp(scores - peak), axis=-1, keepdims=True))
    probs = jnp.exp(scores - logsum).astype(jnp.bfloat16)
    mixed = jnp.einsum("kgqs,skd->qkgd", probs, values, preferred_element_type=jnp.float32)
    output = mixed.reshape(length, heads * HD).astype(jnp.bfloat16)
    saved = (
        query_hat,
        query_scale,
        keys_hat,
        keys_scale,
        turned_query,
        turned_keys,
        values,
        logsum,
    )
    return (output, saved)


def attention_backward(upstream, saved, query_gain, key_gain):
    query_hat, query_scale, keys_hat, keys_scale, turned_query, turned_keys, values, logsum = saved
    length = query_hat.shape[0]
    heads = query_hat.shape[1]
    key_heads = keys_hat.shape[1]
    upstream_b = upstream.astype(jnp.bfloat16).reshape(length, key_heads, heads // key_heads, HD)
    scores = attention_scores(turned_query, turned_keys)
    probs = jnp.exp(scores - logsum)
    probs_b = probs.astype(jnp.bfloat16)
    values_grad = jnp.einsum(
        "kgqs,qkgd->skd", probs_b, upstream_b, preferred_element_type=jnp.float32
    ).astype(jnp.bfloat16)
    probs_grad = jnp.einsum(
        "qkgd,skd->kgqs", upstream_b, values, preferred_element_type=jnp.float32
    )
    delta = jnp.sum(probs * probs_grad, axis=-1, keepdims=True)
    scores_grad = (probs * (probs_grad - delta)).astype(jnp.bfloat16)
    query_group = turned_query.reshape(length, key_heads, heads // key_heads, HD)
    query_back = jnp.einsum(
        "kgqs,skd->qkgd", scores_grad, turned_keys, preferred_element_type=jnp.float32
    ).reshape(length, heads, HD) * HD ** (-0.5)
    keys_back = jnp.einsum(
        "kgqs,qkgd->skd", scores_grad, query_group, preferred_element_type=jnp.float32
    ) * HD ** (-0.5)
    cosine, sine = rope_tables(length)
    query_unspun = query_back * cosine + rotate_back(query_back * sine)
    keys_unspun = keys_back * cosine + rotate_back(keys_back * sine)
    query_grad = head_back(query_unspun, query_hat, query_scale, query_gain).astype(jnp.bfloat16)
    keys_grad = head_back(keys_unspun, keys_hat, keys_scale, key_gain).astype(jnp.bfloat16)
    qgain_grad = jnp.sum(query_unspun * query_hat, axis=(0, 1))
    kgain_grad = jnp.sum(keys_unspun * keys_hat, axis=(0, 1))
    pieces = jnp.concatenate(
        [
            query_grad.reshape(length, -1),
            keys_grad.reshape(length, -1),
            values_grad.reshape(length, -1),
        ],
        axis=1,
    )
    return (pieces, qgain_grad, kgain_grad)


def conv_forward(projected, kernel):
    width = kernel.shape[1]
    length = projected.shape[0]
    gate_in = projected[:, :width]
    gate_out = projected[:, width : 2 * width]
    signal = projected[:, 2 * width :]
    padded = jnp.pad(gate_in * signal, ((KW - 1, 0), (0, 0)))
    convolved = padded[0:length] * kernel[0]
    for offset in range(1, KW):
        convolved = convolved + padded[offset : offset + length] * kernel[offset]
    return ((gate_out * convolved).astype(jnp.bfloat16), convolved, padded)


def conv_backward(upstream, projected, convolved, padded, kernel):
    width = kernel.shape[1]
    length = projected.shape[0]
    gate_in = projected[:, :width]
    gate_out = projected[:, width : 2 * width]
    signal = projected[:, 2 * width :]
    gate_grad = upstream * convolved
    conv_grad = upstream * gate_out
    padded_grad = jnp.pad(conv_grad, ((0, KW - 1), (0, 0)))
    kernel_grad = jnp.stack(
        [jnp.sum(conv_grad * padded[offset : offset + length], axis=0) for offset in range(KW)]
    )
    mixed_grad = padded_grad[KW - 1 : KW - 1 + length] * kernel[0]
    for offset in range(1, KW):
        mixed_grad = (
            mixed_grad + padded_grad[KW - 1 - offset : KW - 1 - offset + length] * kernel[offset]
        )
    pieces = jnp.concatenate([mixed_grad * signal, gate_grad, mixed_grad * gate_in], axis=1).astype(
        jnp.bfloat16
    )
    return (pieces, kernel_grad)


BF = jnp.bfloat16
F32 = jnp.float32


def xor_pairs(count, bits):
    return [(i, i ^ bits) for i in range(count)]


def from_core(x):
    return lax.ppermute(x, "core", xor_pairs(2, 1))


def from_facing(x):
    return lax.ppermute(x, ("xl", "xh"), xor_pairs(4, 3))


def from_xl(x):
    return lax.ppermute(x, "xl", xor_pairs(2, 1))


def from_z(x, bits):
    return lax.ppermute(x, "z", xor_pairs(4, bits))


def from_y(x, bits):
    return lax.ppermute(x, "y", xor_pairs(4, bits))


def gathered(shard):
    facing = from_facing(shard)
    return [shard, from_core(shard), facing, from_core(facing)]


def summed_y(x):
    sent = x.astype(BF)
    total = x
    for bits in (1, 3, 2):
        total = total + from_y(sent, bits).astype(F32)
    return total


def blocks(x):
    width = x.shape[1] // 4
    return [x[:, i * width : (i + 1) * width] for i in range(4)]


def xor_order(parts, index):
    low = (index & 1) == 1
    high = (index & 2) == 2
    a = [jnp.where(low, parts[i ^ 1], parts[i]) for i in range(4)]
    return [jnp.where(high, a[i ^ 2], a[i]) for i in range(4)]


def place():
    row = lax.axis_index("xh") * 2 + lax.axis_index("core")
    return row, lax.axis_index("y")


def spread_in(x):
    row, col = place()
    parts = []
    for bits in range(4):
        pairs = [(w * 4 + s, s * 4 + (w ^ bits)) for w in range(4) for s in range(4)]
        parts.append(lax.ppermute(x, ("xh", "core", "y"), pairs))
    return jnp.concatenate(xor_order(parts, row ^ col), axis=1)


def bring_back(x):
    row, col = place()
    parts = xor_order(blocks(x.astype(BF)), row ^ col)
    total = None
    for bits in range(4):
        pairs = [(s * 4 + c, (c ^ bits) * 4 + s) for s in range(4) for c in range(4)]
        got = lax.ppermute(parts[bits], ("xh", "core", "y"), pairs).astype(F32)
        total = got if total is None else total + got
    return total


def dp_sum(g):
    z = lax.axis_index("z")
    xl = lax.axis_index("xl")
    g = g.astype(BF)
    quarter = g.shape[0] // 4
    half = quarter // 2

    def chunk(at):
        return lax.dynamic_slice_in_dim(g, at * quarter, quarter, 0)

    total = chunk(z).astype(F32)
    for bits in (1, 3, 2):
        total = total + from_z(chunk(z ^ bits), bits).astype(F32)
    sent = lax.dynamic_slice_in_dim(total.astype(BF), (1 - xl) * half, half, 0)
    kept = lax.dynamic_slice_in_dim(total, xl * half, half, 0)
    mine = (kept + from_xl(sent).astype(F32)).astype(BF)
    other = from_xl(mine)
    first = jnp.where(xl == 0, mine, other)
    second = jnp.where(xl == 0, other, mine)
    piece = jnp.concatenate([first, second], axis=0)
    pieces = [piece] + [from_z(piece, bits) for bits in (1, 2, 3)]
    return jnp.concatenate(xor_order(pieces, z), axis=0).astype(F32)


def norm_forward(values, gain):
    scaling = lax.rsqrt(jnp.mean(values * values, axis=1, keepdims=True) + EPS)
    normed = values * scaling
    return (normed, scaling, (normed * gain).astype(BF))


def norm_backward(upstream, normed, scaling, gain):
    scaled_up = upstream * gain
    inner = jnp.mean(scaled_up * normed, axis=1, keepdims=True)
    return scaling * (scaled_up - normed * inner)


def dot(left, right):
    return jnp.dot(left, right, preferred_element_type=F32)


def up(inputs, weights):
    total = None
    for piece, weight in zip(blocks(inputs), weights):
        term = dot(piece, weight)
        total = term if total is None else total + term
    return total


def up_back(upstreams, weight_lists):
    outs = []
    for at in range(4):
        total = None
        for upstream, weights in zip(upstreams, weight_lists):
            term = contract_cols(upstream, weights[at])
            total = term if total is None else total + term
        outs.append(total)
    return jnp.concatenate(outs, axis=1)


def down(hidden, weights):
    return jnp.concatenate([dot(hidden, weight) for weight in weights], axis=1)


def down_back(upstream, weights):
    total = None
    for piece, weight in zip(blocks(upstream), weights):
        term = contract_cols(piece, weight)
        total = term if total is None else total + term
    return total


def four_wide(x):
    facing = from_facing(x)
    return jnp.concatenate([x, from_core(x), facing, from_core(facing)], axis=0)


def four_own(x):
    parts = blocks(x)
    facing = from_facing(jnp.concatenate(parts[2:], axis=1))
    width = parts[0].shape[1]
    return jnp.concatenate(
        [parts[0], from_core(parts[1]), facing[:, :width], from_core(facing[:, width:])], axis=0
    )


def ffn_forward(residual, gain, upper, lower):
    normed, scaling, inputs = norm_forward(residual, gain)
    gating = up(inputs, upper[0])
    upward = up(inputs, upper[1])
    hidden = (jax.nn.silu(gating) * upward).astype(BF)
    return down(hidden, lower), (normed, scaling, inputs, gating, upward, hidden)


def ffn_backward(upstream, saved, gain, upper, lower):
    normed, scaling, inputs, gating, upward, hidden = saved
    cb = upstream.astype(BF)
    hidden_grad = down_back(cb, lower)
    sigmoid = jax.nn.sigmoid(gating)
    gating_grad = (hidden_grad * upward * sigmoid * (1.0 + gating * (1.0 - sigmoid))).astype(BF)
    upward_grad = (hidden_grad * gating * sigmoid).astype(BF)
    normed_grad = up_back([gating_grad, upward_grad], upper)
    gain_grad = jnp.sum(normed_grad * normed, axis=0)
    lower_grad = contract_rows(four_wide(hidden), four_own(cb))
    pieces = jnp.concatenate([gating_grad, upward_grad], axis=1)
    upper_grad = contract_rows(four_own(inputs), four_wide(pieces))
    return norm_backward(normed_grad, normed, scaling, gain), upper_grad, lower_grad, gain_grad


def split_cols(x, count):
    width = x.shape[1] // count
    return jnp.concatenate([x[:, i * width : (i + 1) * width] for i in range(count)], axis=0)


def body(
    stream_in,
    cotangent,
    mixer_gain,
    mixer_input,
    mixer_kernel,
    mixer_output,
    front_gain,
    front_upper,
    front_lower,
    attend_gain,
    attend_query,
    attend_keyval,
    query_gain,
    key_gain,
    attend_output,
    rear_gain,
    rear_upper,
    rear_lower,
):
    gains = jnp.stack([mixer_gain, front_gain, attend_gain, rear_gain])
    gains = jnp.concatenate(gathered(gains), axis=1)
    x = spread_in(stream_in.astype(BF)).astype(F32)
    mi = gathered(mixer_input)
    mo = gathered(mixer_output)
    fu = gathered(front_upper)
    fl = gathered(front_lower)
    aq = gathered(attend_query)
    akv = gathered(attend_keyval)
    ao = gathered(attend_output)
    ru = gathered(rear_upper)
    rl = gathered(rear_lower)
    cot = spread_in(cotangent.astype(BF)).astype(F32)

    def member(lists, at):
        return [w[at] for w in lists]

    fu = [member(fu, 0), member(fu, 1)]
    ru = [member(ru, 0), member(ru, 1)]
    mi = [member(mi, 0), member(mi, 1), member(mi, 2)]
    akv = [member(akv, 0), member(akv, 1)]

    normed_one, scaling_one, inputs_one = norm_forward(x, gains[0])
    projected = jnp.concatenate([up(inputs_one, w) for w in mi], axis=1)
    mixes, convolved, padded = conv_forward(projected, mixer_kernel)
    first = x + summed_y(down(mixes, mo))
    partial, front_saved = ffn_forward(first, gains[1], fu, fl)
    second = first + summed_y(partial)
    normed_three, scaling_three, inputs_three = norm_forward(second, gains[2])
    projected_three = jnp.concatenate([up(inputs_three, w) for w in [aq] + akv], axis=1)
    heads = attend_query.shape[1] // HD
    key_heads = attend_keyval.shape[2] // HD
    attended, attn_saved = attention_forward(
        projected_three, query_gain, key_gain, heads, key_heads
    )
    third = second + summed_y(down(attended, ao))
    partial, rear_saved = ffn_forward(third, gains[3], ru, rl)
    fourth = stream_in + bring_back(partial + 0.25 * (third - x))

    back, rear_upper_grad, rear_lower_grad, rear_gain_grad = ffn_backward(
        cot, rear_saved, gains[3], ru, rl
    )
    rear_upper_grad = dp_sum(split_cols(rear_upper_grad, 2))
    rear_lower_grad = dp_sum(rear_lower_grad)
    third_grad = cot + summed_y(back)
    ab = third_grad.astype(BF)
    attended_grad = down_back(ab, ao)
    attend_output_grad = contract_rows(four_wide(attended), four_own(ab))
    pieces, qgain_grad, kgain_grad = attention_backward(
        attended_grad, attn_saved, query_gain, key_gain
    )
    bounds = [0, heads * HD, (heads + key_heads) * HD, (heads + 2 * key_heads) * HD]
    normed_three_grad = up_back(
        [pieces[:, bounds[i] : bounds[i + 1]] for i in range(3)], [aq] + akv
    )
    attend_gain_grad = jnp.sum(normed_three_grad * normed_three, axis=0)
    second_grad = third_grad + summed_y(
        norm_backward(normed_three_grad, normed_three, scaling_three, gains[2])
    )
    attn_grad = contract_rows(four_own(inputs_three), four_wide(pieces))
    attn_all = dp_sum(jnp.concatenate([split_cols(attn_grad, 2), attend_output_grad], axis=0))
    rows = attend_query.shape[0]
    attend_query_grad = attn_all[:rows]
    keyval_grad = jnp.stack(jnp.split(attn_all[rows : 2 * rows], 2, axis=1))
    attend_output_grad = attn_all[2 * rows :]

    back, front_upper_grad, front_lower_grad, front_gain_grad = ffn_backward(
        second_grad, front_saved, gains[1], fu, fl
    )
    front_upper_grad = dp_sum(split_cols(front_upper_grad, 2))
    front_lower_grad = dp_sum(front_lower_grad)
    first_grad = second_grad + summed_y(back)
    mb = first_grad.astype(BF)
    mixes_grad = down_back(mb, mo)
    mixer_output_grad = dp_sum(contract_rows(four_wide(mixes), four_own(mb)))
    conv_pieces, kernel_grad = conv_backward(mixes_grad, projected, convolved, padded, mixer_kernel)
    width = mixer_kernel.shape[1]
    normed_one_grad = up_back([conv_pieces[:, i * width : (i + 1) * width] for i in range(3)], mi)
    mixer_gain_grad = jnp.sum(normed_one_grad * normed_one, axis=0)
    back = norm_backward(normed_one_grad, normed_one, scaling_one, gains[0])
    stream_grad = cotangent + bring_back(back + 0.25 * (first_grad - cot))
    input_grad = dp_sum(split_cols(contract_rows(four_own(inputs_one), four_wide(conv_pieces)), 3))

    gain_rows = jnp.stack([mixer_gain_grad, front_gain_grad, attend_gain_grad, rear_gain_grad])
    head_row = jnp.pad(jnp.concatenate([qgain_grad, kgain_grad]), (0, width - 2 * HD))[None]
    own, near, far, last = blocks(gain_rows)
    got = from_core(jnp.concatenate([near, last, kernel_grad, head_row], axis=0))
    sums = jnp.concatenate([own, far, kernel_grad, head_row], axis=0) + got
    got = from_facing(sums[4:])
    sums = jnp.concatenate([sums[:4], sums[8:]], axis=0) + got
    sums = sums + from_xl(sums)
    sums = sums + from_z(sums, 1) + from_z(sums, 2) + from_z(sums, 3)
    over_y = jnp.concatenate([sums[:4], sums[7:]], axis=0)
    over_y = over_y + from_y(over_y, 1) + from_y(over_y, 2) + from_y(over_y, 3)
    return (
        fourth,
        stream_grad,
        over_y[0],
        input_grad.reshape(mixer_input.shape),
        sums[4:7],
        mixer_output_grad,
        over_y[1],
        front_upper_grad.reshape(front_upper.shape),
        front_lower_grad,
        over_y[2],
        attend_query_grad,
        keyval_grad,
        over_y[4, :HD],
        over_y[4, HD : 2 * HD],
        attend_output_grad,
        over_y[3],
        rear_upper_grad.reshape(rear_upper.shape),
        rear_lower_grad,
    )


def solution(mesh):
    parts = Mesh(mesh.devices.reshape(4, 2, 2, 2, 4), ("z", "xl", "xh", "core", "y"))
    tokens = ("z", "xl", "y")
    row = ("xh", "core")
    stream = P(tokens, row)
    gain = P(row)
    upper = P(None, row, "y")
    lower = P("y", row)
    weights = (
        gain,
        upper,
        P(None, "y"),
        lower,
        gain,
        upper,
        lower,
        gain,
        P(row, "y"),
        upper,
        P(),
        P(),
        lower,
        gain,
        upper,
        lower,
    )
    return jax.shard_map(
        body,
        mesh=parts,
        in_specs=(stream, stream) + weights,
        out_specs=(stream, stream) + weights,
        check_vma=False,
    )
```

time: 1060 us -> 573 us (0.54)
  waiting for transfers between devices: 679 us -> 230 us
  blocking collectives: 211 us -> 0 us
  starting transfers between devices: 42 us -> 190 us
  matrix products: 40.5 us -> 60.8 us
  local copies, waits for them, and re-layouts: 23.1 us -> 34.4 us
  between operations: 15.2 us -> 4.51 us
    psum x1 -> x0, waiting for transfers between devices: 293 us -> none  [body(): lax.psum((mixer_input_grad, mixer_output_grad, front_upper_grad, front_lo...]
    reduce_scatter x8 -> x0, waiting for transfers between devices: 234 us -> none  [reduce_row(): lax.psum_scatter(rows_of(jnp.int32(0), lax.axis_size('row') * (total_rows...]
    ppermute x0 -> x177, waiting for transfers between devices: none -> 230 us  [the longest x27 87.6 us: from_facing(): return lax.ppermute(x, ('xl', 'xh'), xor_pairs(4, 3))]
    ppermute x0 -> x177, starting transfers between devices: none -> 190 us  [the longest x27 65.9 us: from_facing(): return lax.ppermute(x, ('xl', 'xh'), xor_pairs(4, 3))]
    all_to_all x17 -> x0, blocking collectives: 178 us -> none  [the longest x13 122 us: copy_for_each(): lax.all_to_all(jnp.broadcast_to(x[None], (length, *x.shape)), axis, 0, 0,...]
    all_gather x4 -> x0, waiting for transfers between devices: 84.3 us -> none  [spread_row(): return lax.all_gather(local, 'row', axis=0, tiled=True)]
    all_to_all x11 -> x0, waiting for transfers between devices: 66.7 us -> none  [the longest x7 42 us: copy_for_each(): lax.all_to_all(jnp.broadcast_to(x[None], (length, *x.shape)), axis, 0, 0,...]
    all_to_all x11 -> x0, starting transfers between devices: 41.3 us -> none  [the longest x7 24.8 us: copy_for_each(): lax.all_to_all(jnp.broadcast_to(x[None], (length, *x.shape)), axis, 0, 0,...]
  transfers between devices with their start and end apart: 24 -> 177, of which waited for: 22 -> 66; matrix products, arithmetic and copies ran while one was open for 4% -> 22% of each run, Pallas kernels for 0% -> 0%
where the time goes in v1:
time: 573 us; the launch traced here: 562 us
  waiting for transfers between devices  230 us (40%)
  starting transfers between devices  190 us (33%)
  matrix products  60.8 us (11%)
  other arithmetic  42.1 us (7%)
  local copies, waits for them, and re-layouts  34.4 us (6%)
    ppermute x27, waiting for transfers between devices, from_facing(): return lax.ppermute(x, ('xl', 'xh'), xor_pairs(4, 3))  87.6 us
    ppermute x45, waiting for transfers between devices, from_z(): return lax.ppermute(x, 'z', xor_pairs(4, bits))  72.2 us
    ppermute x27, starting transfers between devices, from_facing(): return lax.ppermute(x, ('xl', 'xh'), xor_pairs(4, 3))  65.9 us
    ppermute x45, starting transfers between devices, from_z(): return lax.ppermute(x, 'z', xor_pairs(4, bits))  55.5 us
    ppermute x15, waiting for transfers between devices, from_xl(): return lax.ppermute(x, 'xl', xor_pairs(2, 1))  34.3 us
    ppermute x21, waiting for transfers between devices, from_y(): return lax.ppermute(x, 'y', xor_pairs(4, bits))  29.1 us
    ppermute x21, starting transfers between devices, from_y(): return lax.ppermute(x, 'y', xor_pairs(4, bits))  27.5 us
    dot_general x56, matrix products, contract_cols(): lax.dot_general(left, right, (((1,), (1,)), ((), ())), preferred_element_...  22.7 us
  transfers between devices with their start and end apart: 177, of which 66 were waited for; matrix products, arithmetic and copies ran while one was open for 22% of the time, Pallas kernels for 0%

profile of v1, /device:TPU:0, one launch (start us, length us, event | category | flops | bytes accessed | tf_op | source)
XLA Modules:
  0.0 562.3 jit_solution(10032382679394672676)
XLA Ops:
  1.5 2.9 collective-permute-start.5
  5.4 3.1 collective-permute-start
  16.4 6.9 %collective-permute-start.48 = (bf16[128,256]{1,0:T(8,128)(2,1)S(1)}, bf16[128,256]{1,0:T(8,128)(2,1)S(1)}, u32[]{:S(2)}, u32[]{:S(2)}) collective-permute-start(bf16[128,256]{1,0:T(8,128)(2,1)S(1)} %convert_element_type.436), channel_id=1, source_target_pairs={{0,2},{1,6},{2,10},{3,14},{4,3},{5,7},{6,11},{7,15},{8,0},{9,4},{1... | collective-permute-start | bytes 196616 | tf_op jit(solution)/shard_map/ppermute | solution.py:242
  24.1 3.1 collective-permute-start.49
  29.2 5.8 %collective-permute-start.8 = (bf16[3,256,256]{2,1,0:T(8,128)(2,1)S(1)}, bf16[3,256,256]{2,1,0:T(8,128)(2,1)S(1)}, u32[]{:S(2)}, u32[]{:S(2)}) collective-permute-start(bf16[3,256,256]{2,1,0:T(8,128)(2,1)S(1)} %copy-done.35), channel_id=1, source_target_pairs={{0,24},{8,16},{16,8},{24,0},{1,25},{9,17},{17,9},{25,1},{2,26},{10... | collective-permute-start | bytes 1179656 | tf_op jit(solution)/shard_map/ppermute | solution.py:192
  35.4 5.5 collective-permute-start.74
  41.6 9.4 %collective-permute-done.74 = bf16[128,512]{1,0:T(8,128)(2,1)S(1)} collective-permute-done((bf16[128,512]{1,0:T(8,128)(2,1)S(1)}, bf16[128,512]{1,0:T(8,128)(2,1)S(1)}, u32[]{:S(2)}, u32[]{:S(2)}) %collective-permute-start.74) | collective-permute-done | bytes 131104 | tf_op jit(solution)/shard_map/ppermute | solution.py:192
  54.0 3.7 collective-permute-done.167
  62.0 11.4 %collective-permute-done.41 = bf16[1152,256]{1,0:T(8,128)(2,1)S(1)} collective-permute-done((bf16[1152,256]{1,0:T(8,128)(2,1)S(1)}, bf16[1152,256]{1,0:T(8,128)(2,1)S(1)}, u32[]{:S(2)}, u32[]{:S(2)}) %collective-permute-start.41) | collective-permute-done | bytes 589856 | tf_op jit(solution)/shard_map/ppermute | solution.py:192
  83.7 6.8 %collective-permute-done.15 = bf16[128,1024]{1,0:T(8,128)(2,1)S(1)} collective-permute-done((bf16[128,1024]{1,0:T(8,128)(2,1)S(1)}, bf16[128,1024]{1,0:T(8,128)(2,1)S(1)}, u32[]{:S(2)}, u32[]{:S(2)}) %collective-permute-start.15) | collective-permute-done | bytes 262176 | tf_op jit(solution)/shard_map/ppermute | solution.py:204
  92.3 3.2 collective-permute-done.14
  99.4 19.5 %collective-permute-done.102 = bf16[128,512]{1,0:T(8,128)(2,1)S(1)} collective-permute-done((bf16[128,512]{1,0:T(8,128)(2,1)S(1)}, bf16[128,512]{1,0:T(8,128)(2,1)S(1)}, u32[]{:S(2)}, u32[]{:S(2)}) %collective-permute-start.102) | collective-permute-done | bytes 131104 | tf_op jit(solution)/shard_map/ppermute | solution.py:192
  131.4 6.1 %collective-permute-done.24 = bf16[128,1024]{1,0:T(8,128)(2,1)S(1)} collective-permute-done((bf16[128,1024]{1,0:T(8,128)(2,1)S(1)}, bf16[128,1024]{1,0:T(8,128)(2,1)S(1)}, u32[]{:S(2)}, u32[]{:S(2)}) %collective-permute-start.24) | collective-permute-done | bytes 262176 | tf_op jit(solution)/shard_map/ppermute | solution.py:204
  137.4 4.8 collective-permute-done.23
  171.9 7.2 %collective-permute-done.38 = bf16[2,256,1152]{2,1,0:T(8,128)(2,1)} collective-permute-done((bf16[2,256,1152]{2,1,0:T(8,128)(2,1)}, bf16[2,256,1152]{2,1,0:T(8,128)(2,1)}, u32[]{:S(2)}, u32[]{:S(2)}) %collective-permute-start.38) | collective-permute-done | bytes 1179680 | tf_op jit(solution)/shard_map/ppermute | solution.py:192
  204.5 5.1 collective-permute-done.46
  209.6 4.0 collective-permute-start.53
  214.2 7.0 %collective-permute-start.150 = (bf16[128,512]{1,0:T(8,128)(2,1)S(1)}, bf16[128,512]{1,0:T(8,128)(2,1)S(1)}, u32[]{:S(2)}, u32[]{:S(2)}) collective-permute-start(bf16[128,512]{1,0:T(8,128)(2,1)S(1)} %concatenate.308), channel_id=1, source_target_pairs={{0,24},{8,16},{16,8},{24,0},{1,25},{9,17},{17,9},{25,1},{2,26},{10... | collective-permute-start | bytes 393224 | tf_op jit(solution)/shard_map/ppermute | solution.py:192
  288.9 3.9 collective-permute-start.143
  295.9 2.7 collective-permute-done.142
  300.1 4.0 collective-permute-done.144
  304.8 4.1 collective-permute-done.145
  316.6 3.2 collective-permute-done.171
  322.8 2.5 collective-permute-start.146
  328.5 2.5 collective-permute-done.57
  340.9 3.1 collective-permute-done.65
  344.0 4.3 collective-permute-done.172
  348.4 3.7 collective-permute-done.66
  352.1 2.5 collective-permute-start.69
  359.8 3.2 collective-permute-start.72
  377.8 4.0 collective-permute-done.123
  381.7 5.3 collective-permute-start.153
  387.1 2.7 collective-permute-start.91
  391.6 2.5 collective-permute-done.173
  394.2 8.0 %collective-permute-done.91 = bf16[128,512]{1,0:T(8,128)(2,1)S(1)} collective-permute-done((bf16[128,512]{1,0:T(8,128)(2,1)S(1)}, bf16[128,512]{1,0:T(8,128)(2,1)S(1)}, u32[]{:S(2)}, u32[]{:S(2)}) %collective-permute-start.91) | collective-permute-done | bytes 131104 | tf_op jit(solution)/shard_map/ppermute | solution.py:192
  403.0 3.5 collective-permute-done.124
  406.6 3.0 collective-permute-start.77
  448.8 14.3 %collective-permute-done.105 = bf16[128,2304]{1,0:T(8,128)(2,1)S(1)} collective-permute-done((bf16[128,2304]{1,0:T(8,128)(2,1)S(1)}, bf16[128,2304]{1,0:T(8,128)(2,1)S(1)}, u32[]{:S(2)}, u32[]{:S(2)}) %collective-permute-start.105) | collective-permute-done | bytes 589856 | tf_op jit(solution)/shard_map/ppermute | solution.py:192
  466.6 2.9 convolution_convert_fusion
  472.9 3.3 collective-permute-done.82
  481.8 7.9 %collective-permute-done.157 = bf16[128,1152]{1,0:T(8,128)(2,1)S(1)} collective-permute-done((bf16[128,1152]{1,0:T(8,128)(2,1)S(1)}, bf16[128,1152]{1,0:T(8,128)(2,1)S(1)}, u32[]{:S(2)}, u32[]{:S(2)}) %collective-permute-start.157) | collective-permute-done | bytes 294944 | tf_op jit(solution)/shard_map/ppermute | solution.py:200
  496.5 4.4 collective-permute-done.85
  503.4 2.9 convolution_convert_fusion.1
  511.9 6.9 %collective-permute-done.109 = bf16[128,1152]{1,0:T(8,128)(2,1)S(1)} collective-permute-done((bf16[128,1152]{1,0:T(8,128)(2,1)S(1)}, bf16[128,1152]{1,0:T(8,128)(2,1)S(1)}, u32[]{:S(2)}, u32[]{:S(2)}) %collective-permute-start.109) | collective-permute-done | bytes 294944 | tf_op jit(solution)/shard_map/ppermute | solution.py:200
  518.9 5.6 collective-permute-done.108
  525.6 5.1 collective-permute-done.110
  538.5 14.0 %collective-permute-done.160 = bf16[128,1152]{1,0:T(8,128)(2,1)S(1)} collective-permute-done((bf16[128,1152]{1,0:T(8,128)(2,1)S(1)}, bf16[128,1152]{1,0:T(8,128)(2,1)S(1)}, u32[]{:S(2)}, u32[]{:S(2)}) %collective-permute-start.160) | collective-permute-done | bytes 294944 | tf_op jit(solution)/shard_map/ppermute | solution.py:200
  554.5 5.0 collective-permute-done.112
  (985 shorter events, 301.4 us)
Async XLA Ops:
  5.4 18.0 %collective-permute-start = (bf16[128,256]{1,0:T(8,128)(2,1)S(1)}, bf16[128,256]{1,0:T(8,128)(2,1)S(1)}, u32[]{:S(2)}, u32[]{:S(2)}) collective-permute-start(bf16[128,256]{1,0:T(8,128)(2,1)S(1)} %convert_element_type.402), channel_id=1, source_target_pairs={{0,3},{1,7},{2,11},{3,15},{4,2},{5,6},{6,10},{7,14},{8,1},{9,5},{1... | collective-permute-start | bytes 196616 | tf_op jit(solution)/shard_map/ppermute | solution.py:242
  27.2 33.2 %collective-permute-start.7 = (bf16[3,256,256]{2,1,0:T(8,128)(2,1)S(1)}, bf16[3,256,256]{2,1,0:T(8,128)(2,1)S(1)}, u32[]{:S(2)}, u32[]{:S(2)}) collective-permute-start(bf16[3,256,256]{2,1,0:T(8,128)(2,1)S(1)} %copy-done.35), channel_id=1, source_target_pairs={{0,4},{4,0},{1,5},{5,1},{2,6},{6,2},{3,7},{7,3},{8,12},{12,8},{9,1... | collective-permute-start | bytes 1179656 | tf_op jit(solution)/shard_map/ppermute | solution.py:188
  29.2 31.5 %collective-permute-start.8 = (bf16[3,256,256]{2,1,0:T(8,128)(2,1)S(1)}, bf16[3,256,256]{2,1,0:T(8,128)(2,1)S(1)}, u32[]{:S(2)}, u32[]{:S(2)}) collective-permute-start(bf16[3,256,256]{2,1,0:T(8,128)(2,1)S(1)} %copy-done.35), channel_id=1, source_target_pairs={{0,24},{8,16},{16,8},{24,0},{1,25},{9,17},{17,9},{25,1},{2,26},{10... | collective-permute-start | bytes 1179656 | tf_op jit(solution)/shard_map/ppermute | solution.py:192
  35.1 38.7 %collective-permute-start.11 = (bf16[256,256]{1,0:T(8,128)(2,1)S(1)}, bf16[256,256]{1,0:T(8,128)(2,1)S(1)}, u32[]{:S(2)}, u32[]{:S(2)}) collective-permute-start(bf16[256,256]{1,0:T(8,128)(2,1)S(1)} %copy-done.85), channel_id=1, source_target_pairs={{0,24},{8,16},{16,8},{24,0},{1,25},{9,17},{17,9},{25,1},{2,26},{10... | collective-permute-start | bytes 393224 | tf_op jit(solution)/shard_map/ppermute | solution.py:192
  35.2 43.2 %collective-permute-start.10 = (bf16[256,256]{1,0:T(8,128)(2,1)S(1)}, bf16[256,256]{1,0:T(8,128)(2,1)S(1)}, u32[]{:S(2)}, u32[]{:S(2)}) collective-permute-start(bf16[256,256]{1,0:T(8,128)(2,1)S(1)} %copy-done.85), channel_id=1, source_target_pairs={{0,4},{4,0},{1,5},{5,1},{2,6},{6,2},{3,7},{7,3},{8,12},{12,8},{9,1... | collective-permute-start | bytes 393224 | tf_op jit(solution)/shard_map/ppermute | solution.py:188
  35.4 15.6 %collective-permute-start.74 = (bf16[128,512]{1,0:T(8,128)(2,1)S(1)}, bf16[128,512]{1,0:T(8,128)(2,1)S(1)}, u32[]{:S(2)}, u32[]{:S(2)}) collective-permute-start(bf16[128,512]{1,0:T(8,128)(2,1)S(1)} %concatenate.302), channel_id=1, source_target_pairs={{0,24},{8,16},{16,8},{24,0},{1,25},{9,17},{17,9},{25,1},{2,26},{10... | collective-permute-start | bytes 393224 | tf_op jit(solution)/shard_map/ppermute | solution.py:192
  57.7 15.7 %collective-permute-start.41 = (bf16[1152,256]{1,0:T(8,128)(2,1)S(1)}, bf16[1152,256]{1,0:T(8,128)(2,1)S(1)}, u32[]{:S(2)}, u32[]{:S(2)}) collective-permute-start(bf16[1152,256]{1,0:T(8,128)(2,1)S(1)} %copy-done.18), channel_id=1, source_target_pairs={{0,24},{8,16},{16,8},{24,0},{1,25},{9,17},{17,9},{25,1},{2,26},{10... | collective-permute-start | bytes 1769480 | tf_op jit(solution)/shard_map/ppermute | solution.py:192
  60.8 59.5 %collective-permute-start.16 = (bf16[2,256,1152]{2,1,0:T(8,128)(2,1)S(1)}, bf16[2,256,1152]{2,1,0:T(8,128)(2,1)S(1)}, u32[]{:S(2)}, u32[]{:S(2)}) collective-permute-start(bf16[2,256,1152]{2,1,0:T(8,128)(2,1)S(1)} %copy-done.4), channel_id=1, source_target_pairs={{0,4},{4,0},{1,5},{5,1},{2,6},{6,2},{3,7},{7,3},{8,12},{12,8},{9,1... | collective-permute-start | bytes 3538952 | tf_op jit(solution)/shard_map/ppermute | solution.py:188
  73.8 45.3 %collective-permute-start.17 = (bf16[2,256,1152]{2,1,0:T(8,128)(2,1)S(1)}, bf16[2,256,1152]{2,1,0:T(8,128)(2,1)S(1)}, u32[]{:S(2)}, u32[]{:S(2)}) collective-permute-start(bf16[2,256,1152]{2,1,0:T(8,128)(2,1)S(1)} %copy-done.4), channel_id=1, source_target_pairs={{0,24},{8,16},{16,8},{24,0},{1,25},{9,17},{17,9},{25,1},{2,26},{10... | collective-permute-start | bytes 3538952 | tf_op jit(solution)/shard_map/ppermute | solution.py:192
  90.5 32.4 %collective-permute-start.20 = (bf16[1152,256]{1,0:T(8,128)(2,1)S(1)}, bf16[1152,256]{1,0:T(8,128)(2,1)S(1)}, u32[]{:S(2)}, u32[]{:S(2)}) collective-permute-start(bf16[1152,256]{1,0:T(8,128)(2,1)S(1)} %copy-done.12), channel_id=1, source_target_pairs={{0,24},{8,16},{16,8},{24,0},{1,25},{9,17},{17,9},{25,1},{2,26},{10... | collective-permute-start | bytes 1769480 | tf_op jit(solution)/shard_map/ppermute | solution.py:192
  95.5 30.6 %collective-permute-start.19 = (bf16[1152,256]{1,0:T(8,128)(2,1)S(1)}, bf16[1152,256]{1,0:T(8,128)(2,1)S(1)}, u32[]{:S(2)}, u32[]{:S(2)}) collective-permute-start(bf16[1152,256]{1,0:T(8,128)(2,1)S(1)} %copy-done.12), channel_id=1, source_target_pairs={{0,4},{4,0},{1,5},{5,1},{2,6},{6,2},{3,7},{7,3},{8,12},{12,8},{9,1... | collective-permute-start | bytes 1769480 | tf_op jit(solution)/shard_map/ppermute | solution.py:188
  96.5 22.5 %collective-permute-start.102 = (bf16[128,512]{1,0:T(8,128)(2,1)S(1)}, bf16[128,512]{1,0:T(8,128)(2,1)S(1)}, u32[]{:S(2)}, u32[]{:S(2)}) collective-permute-start(bf16[128,512]{1,0:T(8,128)(2,1)S(1)} %concatenate.304), channel_id=1, source_target_pairs={{0,24},{8,16},{16,8},{24,0},{1,25},{9,17},{17,9},{25,1},{2,26},{10... | collective-permute-start | bytes 393224 | tf_op jit(solution)/shard_map/ppermute | solution.py:192
  118.9 27.4 %collective-permute-start.25 = (bf16[2,256,128]{2,1,0:T(8,128)(2,1)S(1)}, bf16[2,256,128]{2,1,0:T(8,128)(2,1)S(1)}, u32[]{:S(2)}, u32[]{:S(2)}) collective-permute-start(bf16[2,256,128]{2,1,0:T(8,128)(2,1)S(1)} %copy-done.70), channel_id=1, source_target_pairs={{0,4},{4,0},{1,5},{5,1},{2,6},{6,2},{3,7},{7,3},{8,12},{12,8},{9,1... | collective-permute-start | bytes 393224 | tf_op jit(solution)/shard_map/ppermute | solution.py:188
  120.3 26.1 %collective-permute-start.26 = (bf16[2,256,128]{2,1,0:T(8,128)(2,1)S(1)}, bf16[2,256,128]{2,1,0:T(8,128)(2,1)S(1)}, u32[]{:S(2)}, u32[]{:S(2)}) collective-permute-start(bf16[2,256,128]{2,1,0:T(8,128)(2,1)S(1)} %copy-done.70), channel_id=1, source_target_pairs={{0,24},{8,16},{16,8},{24,0},{1,25},{9,17},{17,9},{25,1},{2,26},{10... | collective-permute-start | bytes 393224 | tf_op jit(solution)/shard_map/ppermute | solution.py:192
  146.3 16.4 %collective-permute-start.31 = (bf16[256,256]{1,0:T(8,128)(2,1)S(1)}, bf16[256,256]{1,0:T(8,128)(2,1)S(1)}, u32[]{:S(2)}, u32[]{:S(2)}) collective-permute-start(bf16[256,256]{1,0:T(8,128)(2,1)S(1)} %copy-done.83), channel_id=1, source_target_pairs={{0,4},{4,0},{1,5},{5,1},{2,6},{6,2},{3,7},{7,3},{8,12},{12,8},{9,1... | collective-permute-start | bytes 393224 | tf_op jit(solution)/shard_map/ppermute | solution.py:188
  149.8 29.4 %collective-permute-start.38 = (bf16[2,256,1152]{2,1,0:T(8,128)(2,1)}, bf16[2,256,1152]{2,1,0:T(8,128)(2,1)}, u32[]{:S(2)}, u32[]{:S(2)}) collective-permute-start(bf16[2,256,1152]{2,1,0:T(8,128)(2,1)} %param.34), channel_id=1, source_target_pairs={{0,24},{8,16},{16,8},{24,0},{1,25},{9,17},{17,9},{25,1},{2,26},{10... | collective-permute-start | bytes 3538952 | tf_op jit(solution)/shard_map/ppermute | solution.py:192
  164.6 16.5 %collective-permute-start.36 = (bf16[128,1024]{1,0:T(8,128)(2,1)}, bf16[128,1024]{1,0:T(8,128)(2,1)}, u32[]{:S(2)}, u32[]{:S(2)}) collective-permute-start(bf16[128,1024]{1,0:T(8,128)(2,1)} %fusion.111), channel_id=1, source_target_pairs={{0,2},{1,3},{2,0},{3,1},{4,6},{5,7},{6,4},{7,5},{8,10},{9,11},{10,... | collective-permute-start | bytes 786440 | tf_op jit(solution)/shard_map/ppermute | solution.py:204
  166.2 17.0 %collective-permute-start.35 = (bf16[128,1024]{1,0:T(8,128)(2,1)}, bf16[128,1024]{1,0:T(8,128)(2,1)S(1)}, u32[]{:S(2)}, u32[]{:S(2)}) collective-permute-start(bf16[128,1024]{1,0:T(8,128)(2,1)} %fusion.111), channel_id=1, source_target_pairs={{0,3},{1,2},{2,1},{3,0},{4,7},{5,6},{6,5},{7,4},{8,11},{9,10},{10,... | collective-permute-start | bytes 786440 | tf_op jit(solution)/shard_map/ppermute | solution.py:204
  167.1 16.1 %collective-permute-start.34 = (bf16[128,1024]{1,0:T(8,128)(2,1)}, bf16[128,1024]{1,0:T(8,128)(2,1)}, u32[]{:S(2)}, u32[]{:S(2)}) collective-permute-start(bf16[128,1024]{1,0:T(8,128)(2,1)} %fusion.111), channel_id=1, source_target_pairs={{0,1},{1,0},{2,3},{3,2},{4,5},{5,4},{6,7},{7,6},{8,9},{9,8},{10,11... | collective-permute-start | bytes 786440 | tf_op jit(solution)/shard_map/ppermute | solution.py:204
  181.1 40.8 %collective-permute-start.136 = (bf16[128,256]{0,1:T(8,128)(2,1)}, bf16[128,256]{0,1:T(8,128)(2,1)}, u32[]{:S(2)}, u32[]{:S(2)}) collective-permute-start(bf16[128,256]{0,1:T(8,128)(2,1)} %bitcast.51), channel_id=1, source_target_pairs={{0,24},{8,16},{16,8},{24,0},{1,25},{9,17},{17,9},{25,1},{2,26},{10... | collective-permute-start | bytes 196616 | tf_op jit(solution)/shard_map/ppermute | solution.py:192
  221.9 35.8 %collective-permute-start.135 = (bf16[128,256]{0,1:T(8,128)(2,1)}, bf16[128,256]{0,1:T(8,128)(2,1)}, u32[]{:S(2)}, u32[]{:S(2)}) collective-permute-start(bf16[128,256]{0,1:T(8,128)(2,1)} %bitcast.51), channel_id=1, source_target_pairs={{0,4},{4,0},{1,5},{5,1},{2,6},{6,2},{3,7},{7,3},{8,12},{12,8},{9,1... | collective-permute-start | bytes 196616 | tf_op jit(solution)/shard_map/ppermute | solution.py:188
  224.1 38.0 %collective-permute-start.137 = (bf16[128,256]{0,1:T(8,128)(2,1)}, bf16[128,256]{0,1:T(8,128)(2,1)}, u32[]{:S(2)}, u32[]{:S(2)}) collective-permute-start(bf16[128,256]{0,1:T(8,128)(2,1)} %collective-permute-done.136), channel_id=1, source_target_pairs={{0,4},{4,0},{1,5},{5,1},{2,6},{6,2},{3,7},{7,3},{8,12},{12,8},{9,1... | collective-permute-start | bytes 196616 | tf_op jit(solution)/shard_map/ppermute | solution.py:188
  250.9 18.5 %collective-permute-start.56 = (bf16[128,1024]{1,0:T(8,128)(2,1)}, bf16[128,1024]{1,0:T(8,128)(2,1)}, u32[]{:S(2)}, u32[]{:S(2)}) collective-permute-start(bf16[128,1024]{1,0:T(8,128)(2,1)} %fusion.311), channel_id=1, source_target_pairs={{0,2},{1,3},{2,0},{3,1},{4,6},{5,7},{6,4},{7,5},{8,10},{9,11},{10,... | collective-permute-start | bytes 786440 | tf_op jit(solution)/shard_map/ppermute | solution.py:204
  252.5 18.9 %collective-permute-start.55 = (bf16[128,1024]{1,0:T(8,128)(2,1)}, bf16[128,1024]{1,0:T(8,128)(2,1)}, u32[]{:S(2)}, u32[]{:S(2)}) collective-permute-start(bf16[128,1024]{1,0:T(8,128)(2,1)} %fusion.311), channel_id=1, source_target_pairs={{0,3},{1,2},{2,1},{3,0},{4,7},{5,6},{6,5},{7,4},{8,11},{9,10},{10,... | collective-permute-start | bytes 786440 | tf_op jit(solution)/shard_map/ppermute | solution.py:204
  265.7 17.7 %collective-permute-start.129 = (bf16[128,256]{1,0:T(8,128)(2,1)}, bf16[128,256]{1,0:T(8,128)(2,1)S(1)}, u32[]{:S(2)}, u32[]{:S(2)}) collective-permute-start(bf16[128,256]{1,0:T(8,128)(2,1)} %get-tuple-element.117), channel_id=1, source_target_pairs={{0,4},{4,0},{1,5},{5,1},{2,6},{6,2},{3,7},{7,3},{8,12},{12,8},{9,1... | collective-permute-start | bytes 196616 | tf_op jit(solution)/shard_map/ppermute | solution.py:188
  287.0 84.0 %collective-permute-start.88 = (bf16[128,256]{1,0:T(8,128)(2,1)S(1)}, bf16[128,256]{1,0:T(8,128)(2,1)}, u32[]{:S(2)}, u32[]{:S(2)}) collective-permute-start(bf16[128,256]{1,0:T(8,128)(2,1)S(1)} %copy-done.34), channel_id=1, source_target_pairs={{0,24},{8,16},{16,8},{24,0},{1,25},{9,17},{17,9},{25,1},{2,26},{10... | collective-permute-start | bytes 196616 | tf_op jit(solution)/shard_map/ppermute | solution.py:192
  295.9 15.8 %collective-permute-start.117 = (bf16[128,1152]{1,0:T(8,128)(2,1)S(1)}, bf16[128,1152]{1,0:T(8,128)(2,1)S(1)}, u32[]{:S(2)}, u32[]{:S(2)}) collective-permute-start(bf16[128,1152]{1,0:T(8,128)(2,1)S(1)} %collective-permute-done.116), channel_id=1, source_target_pairs={{0,4},{4,0},{1,5},{5,1},{2,6},{6,2},{3,7},{7,3},{8,12},{12,8},{9,1... | collective-permute-start | bytes 884744 | tf_op jit(solution)/shard_map/ppermute | solution.py:188
  309.6 16.5 %collective-permute-start.59 = (bf16[128,1024]{1,0:T(8,128)(2,1)S(1)}, bf16[128,1024]{1,0:T(8,128)(2,1)S(1)}, u32[]{:S(2)}, u32[]{:S(2)}) collective-permute-start(bf16[128,1024]{1,0:T(8,128)(2,1)S(1)} %fusion.312), channel_id=1, source_target_pairs={{0,2},{1,3},{2,0},{3,1},{4,6},{5,7},{6,4},{7,5},{8,10},{9,11},{10,... | collective-permute-start | bytes 786440 | tf_op jit(solution)/shard_map/ppermute | solution.py:204
  322.8 29.4 %collective-permute-start.146 = (bf16[192,256]{1,0:T(8,128)(2,1)}, bf16[192,256]{1,0:T(8,128)(2,1)}, u32[]{:S(2)}, u32[]{:S(2)}) collective-permute-start(bf16[192,256]{1,0:T(8,128)(2,1)} %pad_maximum_fusion.26), channel_id=1, source_target_pairs={{0,96},{32,64},{64,32},{96,0},{1,97},{33,65},{65,33},{97,1},{2,98}... | collective-permute-start | bytes 294920 | tf_op jit(solution)/shard_map/ppermute | solution.py:200
  326.1 28.6 %collective-permute-start.147 = (bf16[192,256]{1,0:T(8,128)(2,1)}, bf16[192,256]{1,0:T(8,128)(2,1)}, u32[]{:S(2)}, u32[]{:S(2)}) collective-permute-start(bf16[192,256]{1,0:T(8,128)(2,1)} %pad_maximum_fusion.26), channel_id=1, source_target_pairs={{0,64},{32,96},{64,0},{96,32},{1,65},{33,97},{65,1},{97,33},{2,66}... | collective-permute-start | bytes 294920 | tf_op jit(solution)/shard_map/ppermute | solution.py:200
  328.0 26.7 %collective-permute-start.148 = (bf16[192,256]{1,0:T(8,128)(2,1)}, bf16[192,256]{1,0:T(8,128)(2,1)}, u32[]{:S(2)}, u32[]{:S(2)}) collective-permute-start(bf16[192,256]{1,0:T(8,128)(2,1)} %pad_maximum_fusion.26), channel_id=1, source_target_pairs={{0,32},{32,0},{64,96},{96,64},{1,33},{33,1},{65,97},{97,65},{2,34}... | collective-permute-start | bytes 294920 | tf_op jit(solution)/shard_map/ppermute | solution.py:200
  352.1 21.4 %collective-permute-start.63 = (bf16[128,256]{1,0:T(8,128)(2,1)}, bf16[128,256]{1,0:T(8,128)(2,1)S(1)}, u32[]{:S(2)}, u32[]{:S(2)}) collective-permute-start(bf16[128,256]{1,0:T(8,128)(2,1)} %get-tuple-element.131), channel_id=1, source_target_pairs={{0,12},{1,8},{2,4},{3,0},{4,13},{5,9},{6,5},{7,1},{8,14},{9,10},{1... | collective-permute-start | bytes 196616 | tf_op jit(solution)/shard_map/ppermute | solution.py:252
  371.0 35.5 %collective-permute-start.87 = (bf16[128,256]{1,0:T(8,128)(2,1)S(1)}, bf16[128,256]{1,0:T(8,128)(2,1)S(1)}, u32[]{:S(2)}, u32[]{:S(2)}) collective-permute-start(bf16[128,256]{1,0:T(8,128)(2,1)S(1)} %copy-done.34), channel_id=1, source_target_pairs={{0,4},{4,0},{1,5},{5,1},{2,6},{6,2},{3,7},{7,3},{8,12},{12,8},{9,1... | collective-permute-start | bytes 196616 | tf_op jit(solution)/shard_map/ppermute | solution.py:188
  373.5 36.1 %collective-permute-start.89 = (bf16[128,256]{1,0:T(8,128)(2,1)}, bf16[128,256]{1,0:T(8,128)(2,1)S(1)}, u32[]{:S(2)}, u32[]{:S(2)}) collective-permute-start(bf16[128,256]{1,0:T(8,128)(2,1)} %collective-permute-done.88), channel_id=1, source_target_pairs={{0,4},{4,0},{1,5},{5,1},{2,6},{6,2},{3,7},{7,3},{8,12},{12,8},{9,1... | collective-permute-start | bytes 196616 | tf_op jit(solution)/shard_map/ppermute | solution.py:188
  381.7 64.4 %collective-permute-start.153 = (bf16[128,2304]{1,0:T(8,128)(2,1)S(1)}, bf16[128,2304]{1,0:T(8,128)(2,1)S(1)}, u32[]{:S(2)}, u32[]{:S(2)}) collective-permute-start(bf16[128,2304]{1,0:T(8,128)(2,1)S(1)} %copy-done.63), channel_id=1, source_target_pairs={{0,24},{8,16},{16,8},{24,0},{1,25},{9,17},{17,9},{25,1},{2,26},{10... | collective-permute-start | bytes 1769480 | tf_op jit(solution)/shard_map/ppermute | solution.py:192
  394.1 15.5 %collective-permute-start.90 = (bf16[128,256]{1,0:T(8,128)(2,1)S(1)}, bf16[128,256]{1,0:T(8,128)(2,1)S(1)}, u32[]{:S(2)}, u32[]{:S(2)}) collective-permute-start(bf16[128,256]{1,0:T(8,128)(2,1)S(1)} %copy-done.143), channel_id=1, source_target_pairs={{0,4},{4,0},{1,5},{5,1},{2,6},{6,2},{3,7},{7,3},{8,12},{12,8},{9,1... | collective-permute-start | bytes 196616 | tf_op jit(solution)/shard_map/ppermute | solution.py:188
  406.6 33.7 %collective-permute-start.77 = (bf16[128,768]{1,0:T(8,128)(2,1)S(1)}, bf16[128,768]{1,0:T(8,128)(2,1)S(1)}, u32[]{:S(2)}, u32[]{:S(2)}) collective-permute-start(bf16[128,768]{1,0:T(8,128)(2,1)S(1)} %pad_maximum_fusion.19), channel_id=1, source_target_pairs={{0,24},{8,16},{16,8},{24,0},{1,25},{9,17},{17,9},{25,1},{2,26},{10... | collective-permute-start | bytes 589832 | tf_op jit(solution)/shard_map/ppermute | solution.py:192
  445.6 18.9 %collective-permute-start.152 = (bf16[128,2304]{1,0:T(8,128)(2,1)S(1)}, bf16[128,2304]{1,0:T(8,128)(2,1)S(1)}, u32[]{:S(2)}, u32[]{:S(2)}) collective-permute-start(bf16[128,2304]{1,0:T(8,128)(2,1)S(1)} %copy-done.63), channel_id=1, source_target_pairs={{0,4},{4,0},{1,5},{5,1},{2,6},{6,2},{3,7},{7,3},{8,12},{12,8},{9,1... | collective-permute-start | bytes 1769480 | tf_op jit(solution)/shard_map/ppermute | solution.py:188
  446.2 17.0 %collective-permute-start.151 = (bf16[128,256]{1,0:T(8,128)(2,1)S(1)}, bf16[128,256]{1,0:T(8,128)(2,1)S(1)}, u32[]{:S(2)}, u32[]{:S(2)}) collective-permute-start(bf16[128,256]{1,0:T(8,128)(2,1)S(1)} %copy-done.136), channel_id=1, source_target_pairs={{0,4},{4,0},{1,5},{5,1},{2,6},{6,2},{3,7},{7,3},{8,12},{12,8},{9,1... | collective-permute-start | bytes 196616 | tf_op jit(solution)/shard_map/ppermute | solution.py:188
  446.6 16.5 %collective-permute-start.105 = (bf16[128,2304]{1,0:T(8,128)(2,1)S(1)}, bf16[128,2304]{1,0:T(8,128)(2,1)S(1)}, u32[]{:S(2)}, u32[]{:S(2)}) collective-permute-start(bf16[128,2304]{1,0:T(8,128)(2,1)S(1)} %copy-done.64), channel_id=1, source_target_pairs={{0,24},{8,16},{16,8},{24,0},{1,25},{9,17},{17,9},{25,1},{2,26},{10... | collective-permute-start | bytes 1769480 | tf_op jit(solution)/shard_map/ppermute | solution.py:192
  447.7 18.6 %collective-permute-start.154 = (bf16[128,2304]{1,0:T(8,128)(2,1)S(1)}, bf16[128,2304]{1,0:T(8,128)(2,1)S(1)}, u32[]{:S(2)}, u32[]{:S(2)}) collective-permute-start(bf16[128,2304]{1,0:T(8,128)(2,1)S(1)} %collective-permute-done.153), channel_id=1, source_target_pairs={{0,4},{4,0},{1,5},{5,1},{2,6},{6,2},{3,7},{7,3},{8,12},{12,8},{9,1... | collective-permute-start | bytes 1769480 | tf_op jit(solution)/shard_map/ppermute | solution.py:188
  448.3 55.1 %collective-permute-start.104 = (bf16[128,2304]{1,0:T(8,128)(2,1)S(1)}, bf16[128,2304]{1,0:T(8,128)(2,1)S(1)}, u32[]{:S(2)}, u32[]{:S(2)}) collective-permute-start(bf16[128,2304]{1,0:T(8,128)(2,1)S(1)} %copy-done.64), channel_id=1, source_target_pairs={{0,4},{4,0},{1,5},{5,1},{2,6},{6,2},{3,7},{7,3},{8,12},{12,8},{9,1... | collective-permute-start | bytes 1769480 | tf_op jit(solution)/shard_map/ppermute | solution.py:188
  463.1 40.3 %collective-permute-start.106 = (bf16[128,2304]{1,0:T(8,128)(2,1)S(1)}, bf16[128,2304]{1,0:T(8,128)(2,1)S(1)}, u32[]{:S(2)}, u32[]{:S(2)}) collective-permute-start(bf16[128,2304]{1,0:T(8,128)(2,1)S(1)} %collective-permute-done.105), channel_id=1, source_target_pairs={{0,4},{4,0},{1,5},{5,1},{2,6},{6,2},{3,7},{7,3},{8,12},{12,8},{9,1... | collective-permute-start | bytes 1769480 | tf_op jit(solution)/shard_map/ppermute | solution.py:188
  531.4 21.1 %collective-permute-start.160 = (bf16[128,1152]{1,0:T(8,128)(2,1)S(1)}, bf16[128,1152]{1,0:T(8,128)(2,1)S(1)}, u32[]{:S(2)}, u32[]{:S(2)}) collective-permute-start(bf16[128,1152]{1,0:T(8,128)(2,1)S(1)} %pad_maximum_fusion.15), channel_id=1, source_target_pairs={{0,96},{32,64},{64,32},{96,0},{1,97},{33,65},{65,33},{97,1},{2,98}... | collective-permute-start | bytes 884744 | tf_op jit(solution)/shard_map/ppermute | solution.py:200
  533.1 19.5 %collective-permute-start.161 = (bf16[128,1152]{1,0:T(8,128)(2,1)S(1)}, bf16[128,1152]{1,0:T(8,128)(2,1)S(1)}, u32[]{:S(2)}, u32[]{:S(2)}) collective-permute-start(bf16[128,1152]{1,0:T(8,128)(2,1)S(1)} %pad_maximum_fusion.15), channel_id=1, source_target_pairs={{0,64},{32,96},{64,0},{96,32},{1,65},{33,97},{65,1},{97,33},{2,66}... | collective-permute-start | bytes 884744 | tf_op jit(solution)/shard_map/ppermute | solution.py:200
  534.0 18.6 %collective-permute-start.162 = (bf16[128,1152]{1,0:T(8,128)(2,1)S(1)}, bf16[128,1152]{1,0:T(8,128)(2,1)S(1)}, u32[]{:S(2)}, u32[]{:S(2)}) collective-permute-start(bf16[128,1152]{1,0:T(8,128)(2,1)S(1)} %pad_maximum_fusion.15), channel_id=1, source_target_pairs={{0,32},{32,0},{64,96},{96,64},{1,33},{33,1},{65,97},{97,65},{2,34}... | collective-permute-start | bytes 884744 | tf_op jit(solution)/shard_map/ppermute | solution.py:200
  536.0 23.5 %collective-permute-start.112 = (bf16[128,1152]{1,0:T(8,128)(2,1)S(1)}, bf16[128,1152]{1,0:T(8,128)(2,1)S(1)}, u32[]{:S(2)}, u32[]{:S(2)}) collective-permute-start(bf16[128,1152]{1,0:T(8,128)(2,1)S(1)} %pad_maximum_fusion.14), channel_id=1, source_target_pairs={{0,96},{32,64},{64,32},{96,0},{1,97},{33,65},{65,33},{97,1},{2,98}... | collective-permute-start | bytes 884744 | tf_op jit(solution)/shard_map/ppermute | solution.py:200
  537.6 21.9 %collective-permute-start.113 = (bf16[128,1152]{1,0:T(8,128)(2,1)S(1)}, bf16[128,1152]{1,0:T(8,128)(2,1)S(1)}, u32[]{:S(2)}, u32[]{:S(2)}) collective-permute-start(bf16[128,1152]{1,0:T(8,128)(2,1)S(1)} %pad_maximum_fusion.14), channel_id=1, source_target_pairs={{0,64},{32,96},{64,0},{96,32},{1,65},{33,97},{65,1},{97,33},{2,66}... | collective-permute-start | bytes 884744 | tf_op jit(solution)/shard_map/ppermute | solution.py:200
  (306 other events, 2453.6 us)
